TPU v7x, 256 devices: a whole 4x4x8 slice. The times are simulated.
256 devices in a mesh: row: 64 (over y, x_hi, z), chan: 4 (over x_lo, core).
Axes of the slice: x: 4 (x_hi: 2, x_lo: 2; x = x_hi * 2 + x_lo), y: 4, z: 8, core: 2. Of those that a mesh axis runs over, the one named last changes fastest.
Arguments:
- pair: bfloat16 [512, 512, 128], P('row', 'chan'), may hold values from -6 to 6
- token_mask: int32 [512], replicated, may hold values 0 or 1
- norm_gain: float32 [128], replicated, may hold values from 0.1 to 1.9
- w_a: bfloat16 [128, 128], replicated, may hold values from -0.5 to 0.5
- w_b: bfloat16 [128, 128], replicated, may hold values from -0.5 to 0.5
- w_gate: bfloat16 [128, 128], replicated, may hold values from -0.5 to 0.5
- hid_gain: float32 [64], replicated, may hold values from 0.1 to 1.9
- w_out: bfloat16 [64, 128], replicated, may hold values from -0.75 to 0.75
- cotangent: bfloat16 [512, 512, 128], P('row', 'chan'), may hold values from -6 to 6
Outputs:
- update: bfloat16 [512, 512, 128], P('row', 'chan')
- pair_grad: bfloat16 [512, 512, 128], P('row', 'chan')
All inputs are finite; a program needn't handle non-finite values.
Results may differ from a plain program's by a relative error of at most 0.017.
Values may be sent and summed in bfloat16 or wider, within the bound.
A program may use at most 128 MiB of HBM per device.

v0:
```python
import jax
import jax.numpy as jnp
from jax import lax
from jax.sharding import PartitionSpec as P

epsilon = 1e-05


def layer_norm(values, gains, reduce_dim):
    centered = values - jnp.mean(values, axis=reduce_dim, keepdims=True)
    variance = jnp.mean(centered * centered, axis=reduce_dim, keepdims=True)
    inv_std = lax.rsqrt(variance + epsilon)
    normed = centered * inv_std
    return (normed * gains, normed, inv_std)


def norm_back(gradient, gains, normed, inv_std, reduce_dim):
    scaled = gradient * gains
    mean_one = jnp.mean(scaled, axis=reduce_dim, keepdims=True)
    mean_two = jnp.mean(scaled * normed, axis=reduce_dim, keepdims=True)
    return inv_std * (scaled - mean_one - normed * mean_two)


def gate_forward(projected, hidden, pair_mask):
    sig_gate = jax.nn.sigmoid(projected[:hidden])
    return (sig_gate * projected[hidden:] * pair_mask).astype(jnp.bfloat16)


def gate_back(gradient, projected, hidden, pair_mask):
    sig_gate = jax.nn.sigmoid(projected[:hidden])
    value_part = projected[hidden:]
    masked = gradient * pair_mask
    joined = jnp.concatenate(
        [masked * value_part * sig_gate * (1.0 - sig_gate), masked * sig_gate], axis=0
    )
    return joined.astype(jnp.bfloat16)


def local(pair, token_mask, norm_gain, w_a, w_b, w_gate, hid_gain, w_out, cotangent):
    row_count = pair.shape[0]
    col_count = pair.shape[1]
    hidden = w_out.shape[0]
    row_offset = lax.axis_index("row") * row_count
    col_offset = lax.axis_index("chan") * col_count
    mask_float = token_mask.astype(jnp.float32)
    mask_rows = lax.dynamic_slice_in_dim(mask_float, row_offset, row_count)
    mask_cols = lax.dynamic_slice_in_dim(mask_float, col_offset, col_count)
    pair_mask = mask_rows[:, None] * mask_cols[None, :]
    zn_float, pair_normed, pair_inv = layer_norm(pair.astype(jnp.float32), norm_gain, 2)
    zn = zn_float.astype(jnp.bfloat16)
    proj_a = jnp.einsum("rkc,cg->grk", zn, w_a, preferred_element_type=jnp.float32)
    proj_b = jnp.einsum("rkc,cg->grk", zn, w_b, preferred_element_type=jnp.float32)
    left_col = gate_forward(proj_a, hidden, pair_mask)
    right_col = gate_forward(proj_b, hidden, pair_mask)
    left_hid, right_hid = (
        lax.all_to_all(left_col, "chan", split_axis=0, concat_axis=2, tiled=True),
        lax.all_to_all(right_col, "chan", split_axis=0, concat_axis=2, tiled=True),
    )
    triangle = jnp.einsum(
        "hik,hjk->hij",
        left_hid,
        lax.all_gather(right_hid, "row", axis=1, tiled=True),
        preferred_element_type=jnp.float32,
    )
    tri_col = lax.all_to_all(
        triangle.astype(jnp.bfloat16), "chan", split_axis=2, concat_axis=0, tiled=True
    ).astype(triangle.dtype)
    xn_float, tri_normed, tri_inv = layer_norm(tri_col, hid_gain[:, None, None], 0)
    xn = xn_float.astype(jnp.bfloat16)
    proj_y = jnp.einsum("hrk,hc->rkc", xn, w_out, preferred_element_type=jnp.float32)
    out_gate = jax.nn.sigmoid(
        jnp.einsum("rkc,cd->rkd", zn, w_gate, preferred_element_type=jnp.float32)
    )
    update = (out_gate * proj_y).astype(jnp.bfloat16)
    upstream = cotangent.astype(jnp.float32)
    grad_y = (upstream * out_gate).astype(jnp.bfloat16)
    grad_gate = (upstream * proj_y * out_gate * (1.0 - out_gate)).astype(jnp.bfloat16)
    grad_xn = jnp.einsum("rkc,hc->hrk", grad_y, w_out, preferred_element_type=jnp.float32)
    grad_col = norm_back(grad_xn, hid_gain[:, None, None], tri_normed, tri_inv, 0).astype(
        jnp.bfloat16
    )
    grad_hid = lax.all_to_all(grad_col, "chan", split_axis=0, concat_axis=2, tiled=True)
    grad_cross = lax.all_to_all(grad_hid, "row", split_axis=2, concat_axis=1, tiled=True)
    new_left = jnp.einsum(
        "hij,hjk->hik",
        grad_hid,
        lax.all_gather(right_hid, "row", axis=1, tiled=True),
        preferred_element_type=jnp.float32,
    )
    new_right = jnp.einsum(
        "hij,hik->hjk",
        grad_cross,
        lax.all_gather(left_hid, "row", axis=1, tiled=True),
        preferred_element_type=jnp.float32,
    )
    left_back, right_back = (
        lax.all_to_all(
            new_left.astype(jnp.bfloat16), "chan", split_axis=2, concat_axis=0, tiled=True
        ).astype(new_left.dtype),
        lax.all_to_all(
            new_right.astype(jnp.bfloat16), "chan", split_axis=2, concat_axis=0, tiled=True
        ).astype(new_right.dtype),
    )
    grad_proj_a = gate_back(left_back, proj_a, hidden, pair_mask)
    grad_proj_b = gate_back(right_back, proj_b, hidden, pair_mask)
    grad_zn = jnp.einsum("grk,cg->rkc", grad_proj_a, w_a, preferred_element_type=jnp.float32)
    grad_zn = grad_zn + jnp.einsum(
        "grk,cg->rkc", grad_proj_b, w_b, preferred_element_type=jnp.float32
    )
    grad_zn = grad_zn + jnp.einsum(
        "rkd,cd->rkc", grad_gate, w_gate, preferred_element_type=jnp.float32
    )
    pair_grad = norm_back(grad_zn, norm_gain, pair_normed, pair_inv, 2).astype(jnp.bfloat16)
    return (update, pair_grad)


def solution(mesh):
    in_specs = (P("row", "chan", None), P(), P(), P(), P(), P(), P(), P(), P("row", "chan", None))
    out_specs = (P("row", "chan", None), P("row", "chan", None))
    return jax.shard_map(local, mesh=mesh, in_specs=in_specs, out_specs=out_specs, check_vma=False)
```

profile of v0, /device:TPU:1, one launch (start us, length us, event | category | flops | bytes accessed | tf_op | source)
XLA Modules:
  0.0 371.7 jit_solution(9632143145178823236)
XLA Ops:
  7.2 0.0 copy-start
  7.2 0.0 all-gather.3.cloned.1.call-start
  7.2 1.1 copy.64
  8.4 0.0 copy-start.6
  8.4 0.1 fusion.15
  8.5 1.1 convolution_bitcast_fusion
  9.6 1.1 convolution_bitcast_fusion.1
  10.7 0.7 convert_element_type.91
  11.4 0.1 dynamic_slice.6
  11.5 0.1 dynamic_slice.7
  11.5 0.1 broadcast_multiply_fusion.3
  11.6 0.1 multiply_convert_fusion.8
  11.8 0.1 copy.72
  11.9 9.2 %all_to_all.99 = bf16[64,8,128]{2,1,0:T(8,128)(2,1)S(1)} all-to-all(bf16[64,8,128]{2,1,0:T(8,128)(2,1)S(1)} %copy.72), channel_id=1, replica_groups=mesh['row'=64,'chan'=4] {'chan'}, dimensions={0} | all-to-all | bytes 262144 | tf_op jit(solution)/shard_map/all_to_all | solution.py:57
  21.1 0.7 copy.101
  21.7 0.0 all-gather.3.cloned.1.call-update
  21.8 0.0 all-gather.5.cloned.1.call-start
  21.8 0.1 copy.68
  21.9 7.0 %all_to_all.100 = bf16[64,8,128]{2,1,0:T(8,128)(2,1)S(1)} all-to-all(bf16[64,8,128]{2,1,0:T(8,128)(2,1)S(1)} %copy.68), channel_id=1, replica_groups=mesh['row'=64,'chan'=4] {'chan'}, dimensions={0} | all-to-all | bytes 262144 | tf_op jit(solution)/shard_map/all_to_all | solution.py:56
  28.9 0.7 copy.102
  29.6 0.0 all-gather.5.cloned.1.call-update
  29.6 0.0 copy-start.1
  29.7 0.0 copy-start.5
  29.7 0.0 copy-start.7
  29.7 149.1 %all-gather.3.cloned.1.call-done = bf16[16,512,512]{2,1,0:T(8,128)(2,1)} async-done(((bf16[16,8,512]{2,1,0:T(8,128)(2,1)}), bf16[16,512,512]{2,1,0:T(8,128)(2,1)}) %all-gather.3.cloned.1.call-update) | async-done | bytes 8388624 | tf_op jit(solution)/shard_map/all_gather | solution.py:62
  178.8 5.6 %convolution_convert_fusion.2 = bf16[16,8,512]{2,1,0:T(8,128)(2,1)S(1)} fusion(bf16[16,512,512]{2,1,0:T(8,128)(2,1)} %all-gather.3.cloned.1.call-done, bf16[4,16,8,128]{3,2,1,0:T(8,128)(2,1)S(1)} %bitcast.123), kind=kOutput, calls=%fused_computation.13 | convolution fusion | flops 67174400 | bytes 8650752 | tf_op jit(solution)/shard_map/hik,hjk->hij/dot_general | solution.py:59
  184.4 0.8 copy.74
  185.3 1.7 reshape.100
  187.0 7.0 %all-to-all-start.2 = ((bf16[4,2,8192]{2,1,0:T(2,128)(2,1)}), bf16[4,2,8192]{2,1,0:T(2,128)(2,1)S(1)}, u32[]{:S(2)}, u32[]{:S(2)}) async-start(bf16[4,2,8192]{2,1,0:T(2,128)(2,1)} %reshape.100), calls=%async_computation.2 | async-start | bytes 262144 | tf_op jit(solution)/shard_map/all_to_all | solution.py:65
  194.0 0.4 fusion.2
  194.4 3.2 all-to-all-done.2
  197.6 0.7 reshape.101
  198.3 0.7 copy.75
  199.1 0.2 fusion.55
  199.4 0.1 multiply_convert_fusion.5
  199.5 0.1 copy.76
  199.6 7.0 %all_to_all.101 = bf16[64,8,128]{2,1,0:T(8,128)(2,1)S(1)} all-to-all(bf16[64,8,128]{2,1,0:T(8,128)(2,1)S(1)} %copy.76), channel_id=1, replica_groups=mesh['row'=64,'chan'=4] {'chan'}, dimensions={0} | all-to-all | bytes 262144 | tf_op jit(solution)/shard_map/all_to_all | solution.py:82
  206.6 0.8 copy.80
  207.5 1.8 reshape.104
  209.3 7.3 %all-to-all-start.5 = ((bf16[64,2,512]{2,1,0:T(2,128)(2,1)}), bf16[64,2,512]{2,1,0:T(2,128)(2,1)S(1)}, u32[]{:S(2)}, u32[]{:S(2)}) async-start(bf16[64,2,512]{2,1,0:T(2,128)(2,1)} %reshape.104), calls=%async_computation.5 | async-start | bytes 262144 | tf_op jit(solution)/shard_map/all_to_all | solution.py:83
  216.6 4.6 %convolution_convert_fusion.1 = bf16[16,8,512]{2,1,0:T(8,128)(2,1)S(1)} fusion(bf16[16,512,512]{2,1,0:T(8,128)(2,1)} %all-gather.3.cloned.1.call-done, bf16[4,16,8,128]{3,2,1,0:T(8,128)(2,1)S(1)} %bitcast.121), kind=kOutput, calls=%fused_computation.12 | convolution fusion | flops 67174400 | bytes 8650752 | tf_op jit(solution)/shard_map/hij,hjk->hik/dot_general | solution.py:84
  221.2 0.8 copy.78
  222.0 1.7 reshape.102
  223.7 4.4 %all-to-all-done.5 = bf16[64,2,512]{2,1,0:T(2,128)(2,1)S(1)} async-done(((bf16[64,2,512]{2,1,0:T(2,128)(2,1)}), bf16[64,2,512]{2,1,0:T(2,128)(2,1)S(1)}, u32[]{:S(2)}, u32[]{:S(2)}) %all-to-all-start.5) | async-done | bytes 131104 | tf_op jit(solution)/shard_map/all_to_all | solution.py:83
  228.1 5.7 %all-to-all-start.4 = ((bf16[4,2,8192]{2,1,0:T(2,128)(2,1)}), bf16[4,2,8192]{2,1,0:T(2,128)(2,1)S(1)}, u32[]{:S(2)}, u32[]{:S(2)}) async-start(bf16[4,2,8192]{2,1,0:T(2,128)(2,1)} %reshape.102), calls=%async_computation.4 | async-start | bytes 262144 | tf_op jit(solution)/shard_map/all_to_all | solution.py:97
  233.8 0.7 reshape.105
  234.5 1.3 copy.82
  235.9 2.0 copy.83
  237.9 101.1 %all-gather.5.cloned.1.call-done = bf16[16,512,512]{2,1,0:T(8,128)(2,1)} async-done(((bf16[16,8,512]{2,1,0:T(8,128)(2,1)}), bf16[16,512,512]{2,1,0:T(8,128)(2,1)}) %all-gather.5.cloned.1.call-update) | async-done | bytes 8388624 | tf_op jit(solution)/shard_map/all_gather | solution.py:93
  339.0 4.6 %convolution_convert_fusion = bf16[16,8,512]{2,1,0:T(8,128)(2,1)S(1)} fusion(bf16[16,512,8]{1,2,0:T(8,128)(2,1)S(1)} %copy.83, bf16[16,512,512]{2,1,0:T(8,128)(2,1)} %all-gather.5.cloned.1.call-done), kind=kOutput, calls=%fused_computation.11 | convolution fusion | flops 67174400 | bytes 8650752 | tf_op jit(solution)/shard_map/hij,hik->hjk/dot_general | solution.py:90
  343.5 0.8 copy.84
  344.4 1.7 reshape.106
  346.1 7.6 %all-to-all-start.6 = ((bf16[4,2,8192]{2,1,0:T(2,128)(2,1)}), bf16[4,2,8192]{2,1,0:T(2,128)(2,1)}, u32[]{:S(2)}, u32[]{:S(2)}) async-start(bf16[4,2,8192]{2,1,0:T(2,128)(2,1)} %reshape.106), calls=%async_computation.6 | async-start | bytes 262144 | tf_op jit(solution)/shard_map/all_to_all | solution.py:100
  353.7 1.0 multiply_convert_fusion
  354.7 1.6 reshape.103
  356.3 1.4 copy.79
  357.7 1.6 reshape.107
  359.4 1.4 copy.85
  360.8 1.3 multiply_convert_fusion.2
  362.1 0.2 fusion.28
  362.3 0.2 convolution_add_fusion
  362.5 1.3 fusion.54
  363.8 0.2 fusion.14
  364.0 0.8 copy.86
  (24 shorter events, 0.2 us)
Async XLA Ops:
  7.2 186.8 %copy-start = (bf16[128,128]{1,0:T(8,128)(2,1)S(1)}, bf16[128,128]{1,0:T(8,128)(2,1)}, u32[]{:S(2)}) copy-start(bf16[128,128]{1,0:T(8,128)(2,1)} %param.14) | copy-start | bytes 98308
  7.2 171.6 %all-gather.3.cloned.1.call-start = ((), (), s32[]{:S(2)}) async-start(), calls=%async_computation.7 | async-start | bytes 8519680 | tf_op jit(solution)/shard_map/all_gather | solution.py:62
  8.4 185.7 %copy-start.6 = (f32[128]{0:T(128)S(1)}, f32[128]{0:T(128)}, u32[]{:S(2)}) copy-start(f32[128]{0:T(128)} %param.11) | copy-start | bytes 1540
  21.8 317.2 %all-gather.5.cloned.1.call-start = ((), (), s32[]{:S(2)}) async-start(), calls=%async_computation.8 | async-start | bytes 8519680 | tf_op jit(solution)/shard_map/all_gather | solution.py:93
  29.6 169.5 %copy-start.1 = (bf16[8,128,128]{2,1,0:T(8,128)(2,1)S(1)}, bf16[8,128,128]{2,1,0:T(8,128)(2,1)}, u32[]{:S(2)}) copy-start(bf16[8,128,128]{2,1,0:T(8,128)(2,1)} %param.17) | copy-start | bytes 786436
  29.7 169.5 %copy-start.5 = (bf16[64,128]{1,0:T(8,128)(2,1)S(1)}, bf16[64,128]{1,0:T(8,128)(2,1)}, u32[]{:S(2)}) copy-start(bf16[64,128]{1,0:T(8,128)(2,1)} %param.16) | copy-start | bytes 49156
  29.7 169.5 %copy-start.7 = (f32[64]{0:T(128)S(1)}, f32[64]{0:T(128)}, u32[]{:S(2)}) copy-start(f32[64]{0:T(128)} %param.15) | copy-start | bytes 772
  187.0 10.6 %all-to-all-start.2 = ((bf16[4,2,8192]{2,1,0:T(2,128)(2,1)}), bf16[4,2,8192]{2,1,0:T(2,128)(2,1)S(1)}, u32[]{:S(2)}, u32[]{:S(2)}) async-start(bf16[4,2,8192]{2,1,0:T(2,128)(2,1)} %reshape.100), calls=%async_computation.2 | async-start | bytes 262144 | tf_op jit(solution)/shard_map/all_to_all | solution.py:65
  209.3 18.9 %all-to-all-start.5 = ((bf16[64,2,512]{2,1,0:T(2,128)(2,1)}), bf16[64,2,512]{2,1,0:T(2,128)(2,1)S(1)}, u32[]{:S(2)}, u32[]{:S(2)}) async-start(bf16[64,2,512]{2,1,0:T(2,128)(2,1)} %reshape.104), calls=%async_computation.5 | async-start | bytes 262144 | tf_op jit(solution)/shard_map/all_to_all | solution.py:83
  228.1 118.0 %all-to-all-start.4 = ((bf16[4,2,8192]{2,1,0:T(2,128)(2,1)}), bf16[4,2,8192]{2,1,0:T(2,128)(2,1)S(1)}, u32[]{:S(2)}, u32[]{:S(2)}) async-start(bf16[4,2,8192]{2,1,0:T(2,128)(2,1)} %reshape.102), calls=%async_computation.4 | async-start | bytes 262144 | tf_op jit(solution)/shard_map/all_to_all | solution.py:97
  343.5 18.5 %copy-start.3 = (bf16[128,128]{1,0:T(8,128)(2,1)S(1)}, bf16[128,128]{1,0:T(8,128)(2,1)}, u32[]{:S(2)}) copy-start(bf16[128,128]{1,0:T(8,128)(2,1)} %param.12) | copy-start | bytes 98308
  343.5 18.8 %copy-start.4 = (bf16[128,128]{1,0:T(8,128)(2,1)S(1)}, bf16[128,128]{1,0:T(8,128)(2,1)}, u32[]{:S(2)}) copy-start(bf16[128,128]{1,0:T(8,128)(2,1)} %param.13) | copy-start | bytes 98308
  346.1 7.6 %copy-start.2 = (bf16[4,2,8192]{2,1,0:T(2,128)(2,1)}, bf16[4,2,8192]{2,1,0:T(2,128)(2,1)S(1)}, u32[]{:S(2)}) copy-start(bf16[4,2,8192]{2,1,0:T(2,128)(2,1)S(1)} %all-to-all-done.4) | copy-start | bytes 393220
  346.1 11.6 %all-to-all-start.6 = ((bf16[4,2,8192]{2,1,0:T(2,128)(2,1)}), bf16[4,2,8192]{2,1,0:T(2,128)(2,1)}, u32[]{:S(2)}, u32[]{:S(2)}) async-start(bf16[4,2,8192]{2,1,0:T(2,128)(2,1)} %reshape.106), calls=%async_computation.6 | async-start | bytes 262144 | tf_op jit(solution)/shard_map/all_to_all | solution.py:100
Sparse Core Ops, SparseCore 0:
  21.9 156.8 all-gather.2
  182.8 156.1 all-gather.4
where the time goes:
time: 373 us; the launch traced here: 372 us
  waiting for transfers between devices  258 us (69%)
  starting transfers between devices  27.8 us (7%)
  local copies, waits for them, and re-layouts  25.6 us (7%)
  blocking collectives  23.3 us (6%)
  matrix products  20.2 us (5%)
  between operations  14.4 us (4%)
    all_gather x1, waiting for transfers between devices, local(): lax.all_gather(right_hid, 'row', axis=1, tiled=True)  149 us
    all_gather x1, waiting for transfers between devices, local(): lax.all_gather(left_hid, 'row', axis=1, tiled=True)  101 us
    unnamed x26, local copies, waits for them, and re-layouts  13.6 us
    all_to_all x1, blocking collectives, local(): lax.all_to_all(right_col, 'chan', split_axis=0, concat_axis=2, tiled=True)  9.22 us
    all_to_all x1, starting transfers between devices, local(): lax.all_to_all(new_right.astype(jnp.bfloat16), 'chan', split_axis=2, conc...  7.62 us
  transfers between devices with their start and end apart: 6, of which 4 were waited for; matrix products, arithmetic and copies ran while one was open for 10% of the time, Pallas kernels for 0%

commit v1 on v0

--- a/solution.py
+++ b/solution.py
@@ -36,15 +36,18 @@
     return joined.astype(jnp.bfloat16)
 
 
+def over_row(blocks):
+    return lax.all_to_all(blocks, "row", split_axis=0, concat_axis=0, tiled=True)
+
+
 def local(pair, token_mask, norm_gain, w_a, w_b, w_gate, hid_gain, w_out, cotangent):
-    row_count = pair.shape[0]
-    col_count = pair.shape[1]
+    rows, cols = pair.shape[0], pair.shape[1]
     hidden = w_out.shape[0]
-    row_offset = lax.axis_index("row") * row_count
-    col_offset = lax.axis_index("chan") * col_count
+    groups = 64
+    tokens = rows * groups
     mask_float = token_mask.astype(jnp.float32)
-    mask_rows = lax.dynamic_slice_in_dim(mask_float, row_offset, row_count)
-    mask_cols = lax.dynamic_slice_in_dim(mask_float, col_offset, col_count)
+    mask_rows = lax.dynamic_slice_in_dim(mask_float, lax.axis_index("row") * rows, rows)
+    mask_cols = lax.dynamic_slice_in_dim(mask_float, lax.axis_index("chan") * cols, cols)
     pair_mask = mask_rows[:, None] * mask_cols[None, :]
     zn_float, pair_normed, pair_inv = layer_norm(pair.astype(jnp.float32), norm_gain, 2)
     zn = zn_float.astype(jnp.bfloat16)
@@ -52,19 +55,14 @@
     proj_b = jnp.einsum("rkc,cg->grk", zn, w_b, preferred_element_type=jnp.float32)
     left_col = gate_forward(proj_a, hidden, pair_mask)
     right_col = gate_forward(proj_b, hidden, pair_mask)
-    left_hid, right_hid = (
-        lax.all_to_all(left_col, "chan", split_axis=0, concat_axis=2, tiled=True),
-        lax.all_to_all(right_col, "chan", split_axis=0, concat_axis=2, tiled=True),
-    )
-    triangle = jnp.einsum(
-        "hik,hjk->hij",
-        left_hid,
-        lax.all_gather(right_hid, "row", axis=1, tiled=True),
-        preferred_element_type=jnp.float32,
-    )
-    tri_col = lax.all_to_all(
-        triangle.astype(jnp.bfloat16), "chan", split_axis=2, concat_axis=0, tiled=True
-    ).astype(triangle.dtype)
+    both = over_row(jnp.stack([left_col, right_col], axis=1))
+    left = both[:, 0].reshape(tokens, cols)
+    right = both[:, 1].reshape(tokens, cols)
+    partial = jnp.einsum("ik,jk->ij", left, right, preferred_element_type=jnp.float32)
+    partial = partial.astype(jnp.bfloat16).reshape(tokens, 4, cols).transpose(1, 0, 2)
+    parts = lax.all_to_all(partial, "chan", split_axis=0, concat_axis=0, tiled=True)
+    triangle = jnp.sum(parts.astype(jnp.float32), axis=0).astype(jnp.bfloat16)
+    tri_col = over_row(triangle.reshape(groups, rows, cols)).astype(jnp.float32)
     xn_float, tri_normed, tri_inv = layer_norm(tri_col, hid_gain[:, None, None], 0)
     xn = xn_float.astype(jnp.bfloat16)
     proj_y = jnp.einsum("hrk,hc->rkc", xn, w_out, preferred_element_type=jnp.float32)
@@ -79,30 +77,24 @@
     grad_col = norm_back(grad_xn, hid_gain[:, None, None], tri_normed, tri_inv, 0).astype(
         jnp.bfloat16
     )
-    grad_hid = lax.all_to_all(grad_col, "chan", split_axis=0, concat_axis=2, tiled=True)
-    grad_cross = lax.all_to_all(grad_hid, "row", split_axis=2, concat_axis=1, tiled=True)
+    grad_hid = over_row(grad_col).reshape(1, tokens, cols)
+    spread = jnp.broadcast_to(grad_hid, (4, tokens, cols))
+    grad_all = lax.all_to_all(spread, "chan", split_axis=0, concat_axis=0, tiled=True)
+    right_blocks = right.reshape(4, cols, cols)
     new_left = jnp.einsum(
-        "hij,hjk->hik",
-        grad_hid,
-        lax.all_gather(right_hid, "row", axis=1, tiled=True),
-        preferred_element_type=jnp.float32,
+        "cij,cjk->ik", grad_all, right_blocks, preferred_element_type=jnp.float32
     )
-    new_right = jnp.einsum(
-        "hij,hik->hjk",
-        grad_cross,
-        lax.all_gather(left_hid, "row", axis=1, tiled=True),
-        preferred_element_type=jnp.float32,
+    new_right = jnp.einsum("cij,ik->cjk", grad_all, left, preferred_element_type=jnp.float32)
+    back = jnp.stack(
+        [
+            new_left.astype(jnp.bfloat16).reshape(groups, rows, cols),
+            new_right.astype(jnp.bfloat16).reshape(groups, rows, cols),
+        ],
+        axis=1,
     )
-    left_back, right_back = (
-        lax.all_to_all(
-            new_left.astype(jnp.bfloat16), "chan", split_axis=2, concat_axis=0, tiled=True
-        ).astype(new_left.dtype),
-        lax.all_to_all(
-            new_right.astype(jnp.bfloat16), "chan", split_axis=2, concat_axis=0, tiled=True
-        ).astype(new_right.dtype),
-    )
-    grad_proj_a = gate_back(left_back, proj_a, hidden, pair_mask)
-    grad_proj_b = gate_back(right_back, proj_b, hidden, pair_mask)
+    back = over_row(back).astype(jnp.float32)
+    grad_proj_a = gate_back(back[:, 0], proj_a, hidden, pair_mask)
+    grad_proj_b = gate_back(back[:, 1], proj_b, hidden, pair_mask)
     grad_zn = jnp.einsum("grk,cg->rkc", grad_proj_a, w_a, preferred_element_type=jnp.float32)
     grad_zn = grad_zn + jnp.einsum(
         "grk,cg->rkc", grad_proj_b, w_b, preferred_element_type=jnp.float32

time: 373 us -> 118 us (0.32)
  waiting for transfers between devices: 258 us -> 7.32 us
  blocking collectives: 23.3 us -> 89 us
  starting transfers between devices: 27.8 us -> 7.1 us
  local copies, waits for them, and re-layouts: 25.6 us -> 6.98 us
  matrix products: 20.2 us -> 3.94 us
  between operations: 14.4 us -> 0.92 us
    all_gather x2 -> x0, waiting for transfers between devices: 250 us -> none  [the longest x1 149 us: local(): lax.all_gather(right_hid, 'row', axis=1, tiled=True)]
    all_to_all x3 -> x5, blocking collectives: 23.3 us -> 89 us  [the longest x4 75.7 us: over_row(): lax.all_to_all(blocks, 'row', split_axis=0, concat_axis=0, tiled=True)]
    all_to_all x4 -> x1, starting transfers between devices: 27.7 us -> 7.1 us  [local(): lax.all_to_all(spread, 'chan', split_axis=0, concat_axis=0, tiled=True)]
    dot_general x3, matrix products: 14.8 us -> 0.94 us  [the longest x1 0.35 us: local(): jnp.einsum('cij,ik->cjk', grad_all, left, preferred_element_type=jnp.floa...]
    unnamed x26 -> x20, local copies, waits for them, and re-layouts: 13.6 us -> 4.88 us
    convert_element_type x8 -> x0, local copies, waits for them, and re-layouts: 6.17 us -> none  [the longest x2 2.82 us: local(): left_back, right_back = (lax.all_to_all(new_left.astype(jnp.bfloat16), 'c...]
    all_to_all x6 -> x0, local copies, waits for them, and re-layouts: 5.51 us -> none  [the longest x2 3.32 us: local(): lax.all_to_all(grad_hid, 'row', split_axis=2, concat_axis=1, tiled=True)]
    all_to_all x4 -> x1, waiting for transfers between devices: 7.59 us -> 7.32 us  [local(): lax.all_to_all(spread, 'chan', split_axis=0, concat_axis=0, tiled=True)]
  transfers between devices with their start and end apart: 6 -> 1, of which waited for: 4 -> 1; matrix products, arithmetic and copies ran while one was open for 10% -> 1% of each run, Pallas kernels for 0% -> 0%
where the time goes in v1:
time: 118 us; the launch traced here: 116 us
  blocking collectives  89 us (75%)
  waiting for transfers between devices  7.32 us (6%)
  starting transfers between devices  7.1 us (6%)
  local copies, waits for them, and re-layouts  6.98 us (6%)
  matrix products  3.94 us (3%)
    all_to_all x4, blocking collectives, over_row(): lax.all_to_all(blocks, 'row', split_axis=0, concat_axis=0, tiled=True)  75.7 us
    all_to_all x1, blocking collectives, local(): lax.all_to_all(partial, 'chan', split_axis=0, concat_axis=0, tiled=True)  13.3 us
    all_to_all x1, waiting for transfers between devices, local(): lax.all_to_all(spread, 'chan', split_axis=0, concat_axis=0, tiled=True)  7.32 us
    all_to_all x1, starting transfers between devices, local(): lax.all_to_all(spread, 'chan', split_axis=0, concat_axis=0, tiled=True)  7.1 us
    unnamed x20, local copies, waits for them, and re-layouts  4.88 us
  transfers between devices with their start and end apart: 1, of which 1 were waited for; matrix products, arithmetic and copies ran while one was open for 1% of the time, Pallas kernels for 0%

profile of v1, /device:TPU:1, one launch (start us, length us, event | category | flops | bytes accessed | tf_op | source)
XLA Modules:
  0.0 116.4 jit_solution(18237532968496888664)
XLA Ops:
  0.6 0.0 copy-start
  0.7 1.1 copy.34
  1.8 0.0 copy-start.3
  1.9 0.1 fusion.17
  1.9 0.0 copy-start.8
  2.0 0.7 copy-done.8
  2.6 0.1 dynamic_slice.7
  2.7 0.0 copy-start.6
  2.7 0.1 dynamic_slice.6
  2.8 0.0 copy-done.3
  2.8 0.6 copy-done.6
  3.4 0.0 copy-start.4
  3.4 0.3 convolution_bitcast_fusion.1
  3.7 0.5 copy-done.4
  4.1 0.3 convolution_bitcast_fusion
  4.4 0.1 broadcast_multiply_fusion.3
  4.5 0.1 fusion.51
  4.7 0.2 copy.40
  4.9 27.9 %all_to_all.30 = bf16[64,2,8,128]{3,2,1,0:T(8,128)(2,1)S(1)} all-to-all(bf16[64,2,8,128]{3,2,1,0:T(8,128)(2,1)S(1)} %copy.40), channel_id=1, replica_groups=mesh['row'=64,'chan'=4] {'row'}, dimensions={0} | all-to-all | bytes 524288 | tf_op jit(solution)/shard_map/all_to_all | solution.py:40
  32.8 0.3 convolution_convert_fusion
  33.1 13.3 %all_to_all.31 = bf16[4,512,128]{1,2,0:T(8,128)(2,1)S(1)} all-to-all(bf16[4,512,128]{1,2,0:T(8,128)(2,1)S(1)} %bitcast.88), channel_id=1, replica_groups=mesh['row'=64,'chan'=4] {'chan'}, dimensions={0} | all-to-all | bytes 1048576 | tf_op jit(solution)/shard_map/all_to_all | solution.py:63
  46.4 0.1 reduce_sum.86
  46.4 0.1 copy.43
  46.6 15.5 %all_to_all.32 = bf16[64,8,128]{2,1,0:T(8,128)(2,1)S(1)} all-to-all(bf16[64,8,128]{2,1,0:T(8,128)(2,1)S(1)} %bitcast.90), channel_id=1, replica_groups=mesh['row'=64,'chan'=4] {'row'}, dimensions={0} | all-to-all | bytes 262144 | tf_op jit(solution)/shard_map/all_to_all | solution.py:40
  62.1 0.0 copy-start.5
  62.2 0.0 copy-start.7
  62.2 0.6 copy-done.5
  62.8 0.0 copy-done.7
  62.8 0.3 fusion.53
  63.2 0.0 copy-done
  63.2 0.0 copy-start.1
  63.2 1.1 multiply_convert_fusion
  64.3 0.0 copy-done.1
  64.3 0.2 fusion.80
  64.5 0.1 fusion.31
  64.6 0.1 copy.45
  64.7 15.5 %all_to_all.33 = bf16[64,8,128]{2,1,0:T(8,128)(2,1)S(1)} all-to-all(bf16[64,8,128]{2,1,0:T(8,128)(2,1)S(1)} %copy.45), channel_id=1, replica_groups=mesh['row'=64,'chan'=4] {'row'}, dimensions={0} | all-to-all | bytes 262144 | tf_op jit(solution)/shard_map/all_to_all | solution.py:40
  80.2 0.9 broadcast_in_dim.5
  81.1 7.1 %all-to-all-start.4 = ((bf16[4,512,128]{2,1,0:T(8,128)(2,1)}), bf16[4,512,128]{2,1,0:T(8,128)(2,1)S(1)}, u32[]{:S(2)}, u32[]{:S(2)}) async-start(bf16[4,512,128]{2,1,0:T(8,128)(2,1)} %broadcast_in_dim.5), calls=%async_computation.4 | async-start | bytes 1048576 | tf_op jit(solution)/shard_map/all_to_all | solution.py:82
  88.2 0.7 slice.41
  88.8 7.3 %all-to-all-done.4 = bf16[4,512,128]{2,1,0:T(8,128)(2,1)S(1)} async-done(((bf16[4,512,128]{2,1,0:T(8,128)(2,1)}), bf16[4,512,128]{2,1,0:T(8,128)(2,1)S(1)}, u32[]{:S(2)}, u32[]{:S(2)}) %all-to-all-start.4) | async-done | bytes 524320 | tf_op jit(solution)/shard_map/all_to_all | solution.py:82
  96.2 0.0 copy-start.2
  96.2 0.3 convolution_convert_fusion.1
  96.5 0.6 copy-done.2
  97.1 0.3 fusion.6
  97.5 16.8 %all_to_all.34 = bf16[64,2,8,128]{3,2,1,0:T(8,128)(2,1)S(1)} all-to-all(bf16[64,2,8,128]{3,2,1,0:T(8,128)(2,1)S(1)} %copy.47), channel_id=1, replica_groups=mesh['row'=64,'chan'=4] {'row'}, dimensions={0} | all-to-all | bytes 524288 | tf_op jit(solution)/shard_map/all_to_all | solution.py:40
  114.3 0.1 copy_convert_fusion
  114.3 0.3 multiply_convert_fusion.2
  114.6 0.2 fusion.43
  114.8 0.2 convolution_add_fusion
  115.1 0.3 fusion.79
  115.4 0.2 fusion.16
  115.6 0.9 copy.49
  (14 shorter events, 0.2 us)
Async XLA Ops:
  0.6 62.5 %copy-start = (bf16[128,128]{1,0:T(8,128)(2,1)S(1)}, bf16[128,128]{1,0:T(8,128)(2,1)}, u32[]{:S(2)}) copy-start(bf16[128,128]{1,0:T(8,128)(2,1)} %param.14) | copy-start | bytes 98308
  1.8 0.9 copy-start.3
  1.9 0.7 copy-start.8
  2.7 0.7 copy-start.6
  3.4 0.8 copy-start.4
  62.1 0.7 copy-start.5
  62.2 0.7 copy-start.7
  63.2 1.1 copy-start.1
  81.1 15.1 %all-to-all-start.4 = ((bf16[4,512,128]{2,1,0:T(8,128)(2,1)}), bf16[4,512,128]{2,1,0:T(8,128)(2,1)S(1)}, u32[]{:S(2)}, u32[]{:S(2)}) async-start(bf16[4,512,128]{2,1,0:T(8,128)(2,1)} %broadcast_in_dim.5), calls=%async_computation.4 | async-start | bytes 1048576 | tf_op jit(solution)/shard_map/all_to_all | solution.py:82
  96.2 0.9 copy-start.2

commit v2 on v1

v2 whole, which is shorter than its diff:
```python
import jax
import jax.numpy as jnp
from jax import lax
from jax.experimental import pallas as pl
from jax.experimental.pallas import tpu as pltpu
from jax.sharding import PartitionSpec as P

epsilon = 1e-05
MESH = pl.DeviceIdType.MESH
f32 = jnp.float32
bf16 = jnp.bfloat16


def mean0(values):
    return jnp.sum(values, axis=0, keepdims=True) * (1.0 / values.shape[0])


def mm(a, b):
    return jnp.dot(a, b, preferred_element_type=f32)


def column(row):
    n = row.shape[1]
    same = lax.broadcasted_iota(jnp.int32, (n, n), 0) == lax.broadcasted_iota(jnp.int32, (n, n), 1)
    return jnp.sum(jnp.where(same, row, 0.0), axis=1, keepdims=True)


def kernel(
    pair, mask_s, mask_v, ngain, wa, wb, wg, hgain, wo, cot,
    upd, pgrad,
    wabt, wab, wgt, wot, ng, hg,
    normed, pinv, zn, proj, gate, cgate, qs, mq, xn, gz,
    st_a, st_b, left, right, left_t,
    s1, r1, x1s, x1r, own, s2, r2, s3, r3, gmine, x2r, gl, s4, r4,
    sem_s, sem_r, sem_xs, sem_xr,
):
    rows, cols, feat = pair.shape
    hid = wo.shape[0]
    groups = hid
    tokens = rows * groups
    me = lax.axis_index("row")
    ch = lax.axis_index("chan")
    sib = ch + 1 - 2 * lax.rem(ch, 2)
    peers = [sib, lax.rem(ch + 2, 4), lax.rem(sib + 2, 4)]

    barrier = pltpu.get_barrier_semaphore()

    def greet(s, _):
        pl.semaphore_signal(
            barrier, inc=1, device_id=(lax.rem(me + s, groups), ch), device_id_type=MESH
        )
        return 0

    lax.fori_loop(1, groups, greet, 0)
    for t in peers:
        pl.semaphore_signal(barrier, inc=1, device_id=(me, t), device_id_type=MESH)

    def send_all(src, dst, slot):
        def one(s, _):
            t = lax.rem(me + s, groups)
            pltpu.make_async_remote_copy(
                src.at[t], dst.at[me], sem_s.at[slot], sem_r.at[slot],
                device_id=(t, ch), device_id_type=MESH,
            ).start()
            return 0

        lax.fori_loop(1, groups, one, 0)
        dst[me] = src[me]

    def wait_all(buf, sem):
        part = buf.at[pl.ds(0, groups - 1)]
        pltpu.make_async_copy(part, part, sem).wait()

    def swap(src, dst, which, slot):
        return pltpu.make_async_remote_copy(
            src, dst, sem_xs.at[slot], sem_xr.at[slot],
            device_id=(me, peers[which]), device_id_type=MESH,
        )

    wa_f, wb_f = wa[...].astype(f32), wb[...].astype(f32)
    wabt[0:feat, :] = wa_f.T.astype(bf16)
    wabt[feat : 2 * feat, :] = wb_f.T.astype(bf16)
    wab[:, 0:feat] = wa[...]
    wab[:, feat : 2 * feat] = wb[...]
    ng[...] = jnp.broadcast_to(column(ngain[...]), (feat, cols))
    hg[...] = jnp.broadcast_to(column(hgain[...]), (hid, cols))

    mask_cols = mask_v[pl.ds(ch, 1), :].astype(f32)

    def forward(r, _):
        x = pair[r].astype(f32).T
        centered = x - mean0(x)
        inv = lax.rsqrt(mean0(centered * centered) + epsilon)
        n = centered * inv
        normed[r] = n
        pinv[r] = inv
        z = (n * ng[...]).astype(bf16)
        zn[r] = z
        p = mm(wabt[...], z)
        m = mask_cols * mask_s[me * rows + r].astype(f32)
        sa = jax.nn.sigmoid(p[0:hid])
        sb = jax.nn.sigmoid(p[2 * hid : 3 * hid])
        ma, mb = sa * m, sb * m
        va, vb = p[hid : 2 * hid], p[3 * hid : 4 * hid]
        la, lb = ma * va, mb * vb
        st_a[pl.ds(r, hid, stride=rows), :] = la
        st_b[pl.ds(r, hid, stride=rows), :] = lb
        proj[r, 0:hid] = la * (1.0 - sa)
        proj[r, hid : 2 * hid] = ma
        proj[r, 2 * hid : 3 * hid] = lb * (1.0 - sb)
        proj[r, 3 * hid : 4 * hid] = mb
        return 0

    lax.fori_loop(0, rows, forward, 0)
    s1[:, 0] = st_a[...].reshape(groups, rows, cols).astype(bf16)
    s1[:, 1] = st_b[...].reshape(groups, rows, cols).astype(bf16)
    pl.semaphore_wait(barrier, groups - 1 + 3)
    send_all(s1, r1, 0)

    wgt[...] = wg[...].astype(f32).T.astype(bf16)
    wot[...] = wo[...].astype(f32).T.astype(bf16)

    def gates(r, _):
        g = jax.nn.sigmoid(mm(wgt[...], zn[r]))
        gate[r] = g
        u = cot[r].astype(f32).T * g
        cgate[r] = u * (1.0 - g)
        q = mm(wo[...], u.astype(bf16)) * hg[...]
        qs[r] = q
        mq[r] = mean0(q)
        return 0

    lax.fori_loop(0, rows, gates, 0)

    wait_all(r1, sem_r.at[0])
    left[...] = r1[:, 0].astype(f32).reshape(tokens, cols).astype(bf16)
    right[...] = r1[:, 1].astype(f32).reshape(tokens, cols).astype(bf16)

    def part(t):
        block = right[pl.ds(pl.multiple_of(t * cols, cols), cols), :]
        return lax.dot_general(
            left[...], block, (((1,), (1,)), ((), ())), preferred_element_type=f32
        )

    for w in (2, 1, 0):
        x1s[w] = part(peers[w]).astype(bf16)
        swap(x1s.at[w], x1r.at[w], w, w).start()
    own[...] = part(ch)
    for w in (0, 1, 2):
        swap(x1s.at[w], x1r.at[w], w, w).wait_recv()
    tri = own[...] + x1r[0].astype(f32) + x1r[1].astype(f32) + x1r[2].astype(f32)
    s2[...] = tri.reshape(groups, rows, cols).astype(bf16)
    send_all(s2, r2, 1)
    left_t[...] = left[...].astype(f32).T.astype(bf16)

    wait_all(r2, sem_r.at[1])
    st_a[...] = r2[...].astype(f32).reshape(tokens, cols)

    def middle(r, _):
        t = st_a[pl.ds(r, hid, stride=rows), :]
        centered = t - mean0(t)
        inv = lax.rsqrt(mean0(centered * centered) + epsilon)
        n = centered * inv
        xn[r] = (n * hg[...]).astype(bf16)
        q = qs[r]
        grad = inv * (q - mq[r] - n * mean0(q * n))
        st_b[pl.ds(r, hid, stride=rows), :] = grad
        return 0

    lax.fori_loop(0, rows, middle, 0)
    s3[...] = st_b[...].reshape(groups, rows, cols).astype(bf16)
    send_all(s3, r3, 2)

    def outputs(r, _):
        y = mm(wot[...], xn[r])
        upd[r] = (gate[r] * y).T.astype(bf16)
        gz[r] = mm(wg[...], (cgate[r] * y).astype(bf16))
        return 0

    lax.fori_loop(0, rows, outputs, 0)

    wait_all(r3, sem_r.at[2])
    gmine[...] = r3[...].astype(f32).reshape(tokens, cols).astype(bf16)
    for w in (2, 1, 0):
        swap(gmine, x2r.at[w], w, 3 + w).start()

    def block_grads(grad, t):
        rt = right[pl.ds(pl.multiple_of(t * cols, cols), cols), :]
        right_grad = mm(left_t[...], grad).T
        at = pl.ds(pl.multiple_of(t * (cols // rows), cols // rows), cols // rows)
        s4[at, 1] = right_grad.reshape(cols // rows, rows, cols).astype(bf16)
        return mm(grad, rt)

    gl[...] = block_grads(gmine[...], ch)
    for w in (0, 1, 2):
        swap(gmine, x2r.at[w], w, 3 + w).wait_recv()
        gl[...] += block_grads(x2r[w], peers[w])
    s4[:, 0] = gl[...].reshape(groups, rows, cols).astype(bf16)
    send_all(s4, r4, 3)

    wait_all(r4, sem_r.at[3])
    st_a[...] = r4[:, 0].astype(f32).reshape(tokens, cols)
    st_b[...] = r4[:, 1].astype(f32).reshape(tokens, cols)

    def backward(r, _):
        ga = st_a[pl.ds(r, hid, stride=rows), :]
        gb = st_b[pl.ds(r, hid, stride=rows), :]
        d = (proj[r] * jnp.concatenate([ga, ga, gb, gb], axis=0)).astype(bf16)
        q = (mm(wab[...], d) + gz[r]) * ng[...]
        n = normed[r]
        out = pinv[r] * (q - mean0(q) - n * mean0(q * n))
        pgrad[r] = out.T.astype(bf16)
        return 0

    lax.fori_loop(0, rows, backward, 0)

    for slot, buf in enumerate((s1, s2, s3, s4)):
        wait_all(buf, sem_s.at[slot])
    for w in (0, 1, 2):
        swap(x1s.at[w], x1r.at[w], w, w).wait_send()
        swap(gmine, x2r.at[w], w, 3 + w).wait_send()


def local(pair, token_mask, norm_gain, w_a, w_b, w_gate, hid_gain, w_out, cotangent):
    rows, cols, feat = pair.shape
    hid = w_out.shape[0]
    tokens = token_mask.shape[0]
    groups = tokens // rows
    vm = pl.BlockSpec(memory_space=pltpu.VMEM)
    sm = pl.BlockSpec(memory_space=pltpu.SMEM)
    dma = pltpu.SemaphoreType.DMA

    def V(*shape, dtype=f32):
        return pltpu.VMEM(shape, dtype)

    scratch = [
        V(2 * feat, feat, dtype=bf16), V(feat, 2 * feat, dtype=bf16),
        V(feat, feat, dtype=bf16), V(feat, hid, dtype=bf16),
        V(feat, cols), V(hid, cols),
        V(rows, feat, cols), V(rows, 1, cols), V(rows, feat, cols, dtype=bf16),
        V(rows, 4 * hid, cols), V(rows, feat, cols), V(rows, feat, cols),
        V(rows, hid, cols), V(rows, 1, cols), V(rows, hid, cols, dtype=bf16),
        V(rows, feat, cols),
        V(tokens, cols), V(tokens, cols),
        V(tokens, cols, dtype=bf16), V(tokens, cols, dtype=bf16), V(cols, tokens, dtype=bf16),
        V(groups, 2, rows, cols, dtype=bf16), V(groups, 2, rows, cols, dtype=bf16),
        V(3, tokens, cols, dtype=bf16), V(3, tokens, cols, dtype=bf16), V(tokens, cols),
        V(groups, rows, cols, dtype=bf16), V(groups, rows, cols, dtype=bf16),
        V(groups, rows, cols, dtype=bf16), V(groups, rows, cols, dtype=bf16),
        V(tokens, cols, dtype=bf16), V(3, tokens, cols, dtype=bf16), V(tokens, cols),
        V(groups, 2, rows, cols, dtype=bf16), V(groups, 2, rows, cols, dtype=bf16),
        dma((4,)), dma((4,)), dma((6,)), dma((6,)),
    ]
    out = jax.ShapeDtypeStruct(pair.shape, bf16)
    return pl.pallas_call(
        kernel,
        out_shape=(out, out),
        in_specs=[vm, sm, vm, vm, vm, vm, vm, vm, vm, vm],
        out_specs=(vm, vm),
        scratch_shapes=scratch,
        compiler_params=pltpu.CompilerParams(
            collective_id=0, has_side_effects=True, vmem_limit_bytes=32 << 20
        ),
    )(
        pair, token_mask, token_mask.reshape(tokens // cols, cols), norm_gain.reshape(1, feat),
        w_a, w_b, w_gate, hid_gain.reshape(1, hid), w_out, cotangent,
    )


def solution(mesh):
    in_specs = (P("row", "chan", None), P(), P(), P(), P(), P(), P(), P(), P("row", "chan", None))
    out_specs = (P("row", "chan", None), P("row", "chan", None))
    return jax.shard_map(local, mesh=mesh, in_specs=in_specs, out_specs=out_specs, check_vma=False)
```

time: 118 us -> 71 us (0.60)
  the two profiles are of different devices: /device:TPU:1 before, /device:TPU:2 now
where the time goes in v2:
time: 71 us; the launch traced here: 70.6 us
  Pallas kernels  62.9 us (89%)
  local copies, waits for them, and re-layouts  6.96 us (10%)
    pallas_call x1, Pallas kernels, local(): pl.pallas_call(kernel, out_shape=(out, out), in_specs=[vm, sm, vm, vm, vm...  62.9 us
    unnamed x20, local copies, waits for them, and re-layouts  6.96 us

profile of v2, /device:TPU:2, one launch (start us, length us, event | category | flops | bytes accessed | tf_op | source)
XLA Modules:
  0.0 70.6 jit_solution(17300672308550951365)
XLA Ops:
  0.6 0.0 copy-start.6
  0.6 0.0 copy-start.7
  0.7 0.0 copy-start.8
  0.7 0.7 copy-done.6
  1.3 0.0 copy-done.7
  1.3 0.0 copy-done.8
  1.3 0.0 copy-start
  1.3 0.9 %copy-done = bf16[8,128,128]{2,1,0:T(8,128)(2,1)S(1)} copy-done((bf16[8,128,128]{2,1,0:T(8,128)(2,1)S(1)}, bf16[8,128,128]{2,1,0:T(8,128)(2,1)}, u32[]{:S(2)}) %copy-start) | copy-done | bytes 262168
  2.3 0.0 copy-start.1
  2.3 0.9 %copy-done.1 = bf16[8,128,128]{2,1,0:T(8,128)(2,1)S(1)} copy-done((bf16[8,128,128]{2,1,0:T(8,128)(2,1)S(1)}, bf16[8,128,128]{2,1,0:T(8,128)(2,1)}, u32[]{:S(2)}) %copy-start.1) | copy-done | bytes 262168
  3.2 0.0 copy-start.2
  3.2 0.8 %copy-done.2 = bf16[128,128]{1,0:T(8,128)(2,1)S(1)} copy-done((bf16[128,128]{1,0:T(8,128)(2,1)S(1)}, bf16[128,128]{1,0:T(8,128)(2,1)}, u32[]{:S(2)}) %copy-start.2) | copy-done | bytes 32792
  4.0 0.0 copy-start.3
  4.0 0.8 %copy-done.3 = bf16[128,128]{1,0:T(8,128)(2,1)S(1)} copy-done((bf16[128,128]{1,0:T(8,128)(2,1)S(1)}, bf16[128,128]{1,0:T(8,128)(2,1)}, u32[]{:S(2)}) %copy-start.3) | copy-done | bytes 32792
  4.7 0.0 copy-start.4
  4.7 0.8 %copy-done.4 = bf16[128,128]{1,0:T(8,128)(2,1)S(1)} copy-done((bf16[128,128]{1,0:T(8,128)(2,1)S(1)}, bf16[128,128]{1,0:T(8,128)(2,1)}, u32[]{:S(2)}) %copy-start.4) | copy-done | bytes 32792
  5.5 0.0 copy-start.5
  5.5 0.7 %copy-done.5 = bf16[64,128]{1,0:T(8,128)(2,1)S(1)} copy-done((bf16[64,128]{1,0:T(8,128)(2,1)S(1)}, bf16[64,128]{1,0:T(8,128)(2,1)}, u32[]{:S(2)}) %copy-start.5) | copy-done | bytes 16408
  6.2 62.9 %shard_map.104 = (bf16[8,128,128]{2,1,0:T(8,128)(2,1)S(1)}, bf16[8,128,128]{2,1,0:T(8,128)(2,1)S(1)}) custom-call(bf16[8,128,128]{2,1,0:T(8,128)(2,1)S(1)} %copy-done, s32[512]{0:T(512)S(1)} %copy-done.6, s32[4,128]{1,0:T(4,128)S(1)} %bitcast.3, f32[1,128]{1,0:T(1,128)S(1)} %bitcast.4, bf16[128,128]{1,0:T(8,128)(2,1)S(1)} %copy-done.2, ...), custom_call_target="tpu_custom_call" | custom-call | tf_op jit(solution)/shard_map/pallas_call | solution.py:255
  69.2 0.7 copy.13
  69.9 0.7 copy.14
Async XLA Ops:
  0.6 0.7 copy-start.6
  0.6 0.7 copy-start.7
  0.7 0.7 copy-start.8
  1.3 1.0 %copy-start = (bf16[8,128,128]{2,1,0:T(8,128)(2,1)S(1)}, bf16[8,128,128]{2,1,0:T(8,128)(2,1)}, u32[]{:S(2)}) copy-start(bf16[8,128,128]{2,1,0:T(8,128)(2,1)} %pair.1) | copy-start | bytes 786436
  2.3 0.9 %copy-start.1 = (bf16[8,128,128]{2,1,0:T(8,128)(2,1)S(1)}, bf16[8,128,128]{2,1,0:T(8,128)(2,1)}, u32[]{:S(2)}) copy-start(bf16[8,128,128]{2,1,0:T(8,128)(2,1)} %cot.1) | copy-start | bytes 786436
  3.2 0.8 %copy-start.2 = (bf16[128,128]{1,0:T(8,128)(2,1)S(1)}, bf16[128,128]{1,0:T(8,128)(2,1)}, u32[]{:S(2)}) copy-start(bf16[128,128]{1,0:T(8,128)(2,1)} %wa.1) | copy-start | bytes 98308
  4.0 0.8 %copy-start.3 = (bf16[128,128]{1,0:T(8,128)(2,1)S(1)}, bf16[128,128]{1,0:T(8,128)(2,1)}, u32[]{:S(2)}) copy-start(bf16[128,128]{1,0:T(8,128)(2,1)} %wb.1) | copy-start | bytes 98308
  4.7 0.8 %copy-start.4 = (bf16[128,128]{1,0:T(8,128)(2,1)S(1)}, bf16[128,128]{1,0:T(8,128)(2,1)}, u32[]{:S(2)}) copy-start(bf16[128,128]{1,0:T(8,128)(2,1)} %wg.1) | copy-start | bytes 98308
  5.5 0.7 %copy-start.5 = (bf16[64,128]{1,0:T(8,128)(2,1)S(1)}, bf16[64,128]{1,0:T(8,128)(2,1)}, u32[]{:S(2)}) copy-start(bf16[64,128]{1,0:T(8,128)(2,1)} %wo.1) | copy-start | bytes 49156

commit v3 on v2

--- a/solution.py
+++ b/solution.py
@@ -26,13 +26,14 @@
 
 
 def kernel(
-    pair, mask_s, mask_v, ngain, wa, wb, wg, hgain, wo, cot,
+    pair_h, mask_h, ngain_h, wa_h, wb_h, wg_h, hgain_h, wo_h, cot_h,
     upd, pgrad,
+    pair, mask, ngain, wa, wb, wg, hgain, wo, cot, pmask,
     wabt, wab, wgt, wot, ng, hg,
     normed, pinv, zn, proj, gate, cgate, qs, mq, xn, gz,
     st_a, st_b, left, right, left_t,
-    s1, r1, x1s, x1r, own, s2, r2, s3, r3, gmine, x2r, gl, s4, r4,
-    sem_s, sem_r, sem_xs, sem_xr,
+    s1, r1, x1s, x1r, own, s2, r2, s3, r3, gmine, x2r, gl, s4a, s4b, r4a, r4b,
+    sem_i, sem_s, sem_r, sem_xs, sem_xr,
 ):
     rows, cols, feat = pair.shape
     hid = wo.shape[0]
@@ -41,51 +42,72 @@
     me = lax.axis_index("row")
     ch = lax.axis_index("chan")
     sib = ch + 1 - 2 * lax.rem(ch, 2)
-    peers = [sib, lax.rem(ch + 2, 4), lax.rem(sib + 2, 4)]
+    nei = lax.rem(ch + 2, 4)
+    diag = lax.rem(sib + 2, 4)
+
+    def fetch(i):
+        src = (pair_h, wa_h, wb_h, ngain_h, mask_h, wg_h, wo_h, hgain_h, cot_h)[i]
+        dst = (pair, wa, wb, ngain, mask, wg, wo, hgain, cot)[i]
+        return pltpu.make_async_copy(src, dst, sem_i.at[i])
+
+    for i in range(9):
+        fetch(i).start()
+
+    def far(u):
+        iz, iy, ix = u % 8, u // 8 % 4, u // 32
+        dz = 4 + (iz + 1) // 2 * (1 - 2 * (iz % 2))
+        dy = 2 + (iy + 1) // 2 * (1 - 2 * (iy % 2))
+        return (me // 16 + dy) % 4 * 16 + (me // 8 + 1 - ix) % 2 * 8 + (me % 8 + dz) % 8
 
     barrier = pltpu.get_barrier_semaphore()
 
     def greet(s, _):
         pl.semaphore_signal(
-            barrier, inc=1, device_id=(lax.rem(me + s, groups), ch), device_id_type=MESH
+            barrier, inc=1, device_id=(far(s), ch), device_id_type=MESH
         )
         return 0
 
-    lax.fori_loop(1, groups, greet, 0)
-    for t in peers:
+    lax.fori_loop(0, groups - 1, greet, 0)
+    for t in (sib, nei):
         pl.semaphore_signal(barrier, inc=1, device_id=(me, t), device_id_type=MESH)
 
     def send_all(src, dst, slot):
         def one(s, _):
-            t = lax.rem(me + s, groups)
+            t = far(s)
             pltpu.make_async_remote_copy(
                 src.at[t], dst.at[me], sem_s.at[slot], sem_r.at[slot],
                 device_id=(t, ch), device_id_type=MESH,
             ).start()
             return 0
 
-        lax.fori_loop(1, groups, one, 0)
+        lax.fori_loop(0, groups - 1, one, 0)
         dst[me] = src[me]
 
     def wait_all(buf, sem):
         part = buf.at[pl.ds(0, groups - 1)]
         pltpu.make_async_copy(part, part, sem).wait()
 
-    def swap(src, dst, which, slot):
+    def swap(src, dst, to, slot):
         return pltpu.make_async_remote_copy(
             src, dst, sem_xs.at[slot], sem_xr.at[slot],
-            device_id=(me, peers[which]), device_id_type=MESH,
+            device_id=(me, to), device_id_type=MESH,
         )
 
+    for i in range(5):
+        fetch(i).wait()
     wa_f, wb_f = wa[...].astype(f32), wb[...].astype(f32)
     wabt[0:feat, :] = wa_f.T.astype(bf16)
     wabt[feat : 2 * feat, :] = wb_f.T.astype(bf16)
     wab[:, 0:feat] = wa[...]
     wab[:, feat : 2 * feat] = wb[...]
     ng[...] = jnp.broadcast_to(column(ngain[...]), (feat, cols))
-    hg[...] = jnp.broadcast_to(column(hgain[...]), (hid, cols))
-
-    mask_cols = mask_v[pl.ds(ch, 1), :].astype(f32)
+    place = lax.broadcasted_iota(jnp.int32, (rows, cols), 1)
+    step = lax.broadcasted_iota(jnp.int32, (rows, cols), 0)
+    near = mask[pl.ds(me * rows // cols, 1), :].astype(f32)
+    mask_rows = jnp.sum(
+        jnp.where(place == step + me * rows % cols, near, 0.0), axis=1, keepdims=True
+    )
+    pmask[...] = mask_rows * mask[pl.ds(ch, 1), :].astype(f32)
 
     def forward(r, _):
         x = pair[r].astype(f32).T
@@ -97,7 +119,7 @@
         z = (n * ng[...]).astype(bf16)
         zn[r] = z
         p = mm(wabt[...], z)
-        m = mask_cols * mask_s[me * rows + r].astype(f32)
+        m = pmask[pl.ds(r, 1), :]
         sa = jax.nn.sigmoid(p[0:hid])
         sb = jax.nn.sigmoid(p[2 * hid : 3 * hid])
         ma, mb = sa * m, sb * m
@@ -114,9 +136,12 @@
     lax.fori_loop(0, rows, forward, 0)
     s1[:, 0] = st_a[...].reshape(groups, rows, cols).astype(bf16)
     s1[:, 1] = st_b[...].reshape(groups, rows, cols).astype(bf16)
-    pl.semaphore_wait(barrier, groups - 1 + 3)
+    pl.semaphore_wait(barrier, groups - 1 + 2)
     send_all(s1, r1, 0)
 
+    for i in range(5, 9):
+        fetch(i).wait()
+    hg[...] = jnp.broadcast_to(column(hgain[...]), (hid, cols))
     wgt[...] = wg[...].astype(f32).T.astype(bf16)
     wot[...] = wo[...].astype(f32).T.astype(bf16)
 
@@ -142,13 +167,18 @@
             left[...], block, (((1,), (1,)), ((), ())), preferred_element_type=f32
         )
 
-    for w in (2, 1, 0):
-        x1s[w] = part(peers[w]).astype(bf16)
-        swap(x1s.at[w], x1r.at[w], w, w).start()
+    for w, t in enumerate((diag, sib)):
+        x1s[w] = part(t).astype(bf16)
+        swap(x1s.at[w], x1r.at[w], sib, w).start()
+    own[...] = part(nei)
+    swap(x1s.at[0], x1r.at[0], sib, 0).wait_recv()
+    x1s[2] = (own[...] + x1r[0].astype(f32)).astype(bf16)
+    swap(x1s.at[2], x1r.at[2], nei, 2).start()
     own[...] = part(ch)
-    for w in (0, 1, 2):
-        swap(x1s.at[w], x1r.at[w], w, w).wait_recv()
-    tri = own[...] + x1r[0].astype(f32) + x1r[1].astype(f32) + x1r[2].astype(f32)
+    swap(x1s.at[1], x1r.at[1], sib, 1).wait_recv()
+    own[...] += x1r[1].astype(f32)
+    swap(x1s.at[2], x1r.at[2], nei, 2).wait_recv()
+    tri = own[...] + x1r[2].astype(f32)
     s2[...] = tri.reshape(groups, rows, cols).astype(bf16)
     send_all(s2, r2, 1)
     left_t[...] = left[...].astype(f32).T.astype(bf16)
@@ -181,26 +211,63 @@
 
     wait_all(r3, sem_r.at[2])
     gmine[...] = r3[...].astype(f32).reshape(tokens, cols).astype(bf16)
-    for w in (2, 1, 0):
-        swap(gmine, x2r.at[w], w, 3 + w).start()
-
-    def block_grads(grad, t):
-        rt = right[pl.ds(pl.multiple_of(t * cols, cols), cols), :]
-        right_grad = mm(left_t[...], grad).T
-        at = pl.ds(pl.multiple_of(t * (cols // rows), cols // rows), cols // rows)
-        s4[at, 1] = right_grad.reshape(cols // rows, rows, cols).astype(bf16)
-        return mm(grad, rt)
-
-    gl[...] = block_grads(gmine[...], ch)
-    for w in (0, 1, 2):
-        swap(gmine, x2r.at[w], w, 3 + w).wait_recv()
-        gl[...] += block_grads(x2r[w], peers[w])
-    s4[:, 0] = gl[...].reshape(groups, rows, cols).astype(bf16)
-    send_all(s4, r4, 3)
-
-    wait_all(r4, sem_r.at[3])
-    st_a[...] = r4[:, 0].astype(f32).reshape(tokens, cols)
-    st_b[...] = r4[:, 1].astype(f32).reshape(tokens, cols)
+    half = tokens // 2
+    parts = (pl.ds(0, half), pl.ds(half, half))
+
+    def onward(k):
+        return swap(gmine.at[parts[k]], x2r.at[1, parts[k]], nei, 4 + k)
+
+    def relay(k):
+        return swap(x2r.at[1, parts[k]], x2r.at[2, parts[k]], sib, 6 + k)
+
+    onward(0).start()
+    onward(1).start()
+    swap(gmine, x2r.at[0], sib, 3).start()
+    span = cols // rows
+
+    def right_grads(grad, t):
+        block = mm(left_t[...], grad).T
+        s4b[pl.ds(t * span, span)] = block.reshape(span, rows, cols).astype(bf16)
+
+        def one(u, _):
+            to = t * span + (me + span // 2 + u) % span
+
+            @pl.when(to != me)
+            def _():
+                pltpu.make_async_remote_copy(
+                    s4b.at[to], r4b.at[me], sem_s.at[4], sem_r.at[4],
+                    device_id=(to, ch), device_id_type=MESH,
+                ).start()
+
+            return 0
+
+        lax.fori_loop(0, span, one, 0)
+
+    def left_grads(grad, t):
+        return mm(grad, right[pl.ds(pl.multiple_of(t * cols, cols), cols), :])
+
+    gl[...] = left_grads(gmine[...], ch)
+    right_grads(gmine[...], ch)
+    swap(gmine, x2r.at[0], sib, 3).wait_recv()
+    gl[...] += left_grads(x2r[0], sib)
+    right_grads(x2r[0], sib)
+    for k in (0, 1):
+        onward(k).wait_recv()
+        relay(k).start()
+    gl[...] += left_grads(x2r[1], nei)
+    right_grads(x2r[1], nei)
+    for k in (0, 1):
+        relay(k).wait_recv()
+    last = gl[...] + left_grads(x2r[2], diag)
+    s4a[...] = last.reshape(groups, rows, cols).astype(bf16)
+    send_all(s4a, r4a, 3)
+    right_grads(x2r[2], diag)
+    r4b[me] = s4b[me]
+
+    wait_all(r4a, sem_r.at[3])
+    st_a[...] = r4a[...].astype(f32).reshape(tokens, cols)
+    wait_all(r4b, sem_r.at[4])
+    st_b[...] = r4b[...].astype(f32).reshape(tokens, cols)
 
     def backward(r, _):
         ga = st_a[pl.ds(r, hid, stride=rows), :]
@@ -214,11 +281,15 @@
 
     lax.fori_loop(0, rows, backward, 0)
 
-    for slot, buf in enumerate((s1, s2, s3, s4)):
+    for slot, buf in enumerate((s1, s2, s3, s4a, s4b)):
         wait_all(buf, sem_s.at[slot])
-    for w in (0, 1, 2):
-        swap(x1s.at[w], x1r.at[w], w, w).wait_send()
-        swap(gmine, x2r.at[w], w, 3 + w).wait_send()
+    for w in (0, 1):
+        swap(x1s.at[w], x1r.at[w], sib, w).wait_send()
+    swap(x1s.at[2], x1r.at[2], nei, 2).wait_send()
+    swap(gmine, x2r.at[0], sib, 3).wait_send()
+    for k in (0, 1):
+        onward(k).wait_send()
+        relay(k).wait_send()
 
 
 def local(pair, token_mask, norm_gain, w_a, w_b, w_gate, hid_gain, w_out, cotangent):
@@ -227,13 +298,16 @@
     tokens = token_mask.shape[0]
     groups = tokens // rows
     vm = pl.BlockSpec(memory_space=pltpu.VMEM)
-    sm = pl.BlockSpec(memory_space=pltpu.SMEM)
+    hbm = pl.BlockSpec(memory_space=pl.ANY)
     dma = pltpu.SemaphoreType.DMA
 
     def V(*shape, dtype=f32):
         return pltpu.VMEM(shape, dtype)
 
     scratch = [
+        V(rows, cols, feat, dtype=bf16), V(tokens // cols, cols, dtype=jnp.int32), V(1, feat),
+        V(feat, 2 * hid, dtype=bf16), V(feat, 2 * hid, dtype=bf16), V(feat, feat, dtype=bf16),
+        V(1, hid), V(hid, feat, dtype=bf16), V(rows, cols, feat, dtype=bf16), V(rows, cols),
         V(2 * feat, feat, dtype=bf16), V(feat, 2 * feat, dtype=bf16),
         V(feat, feat, dtype=bf16), V(feat, hid, dtype=bf16),
         V(feat, cols), V(hid, cols),
@@ -248,21 +322,22 @@
         V(groups, rows, cols, dtype=bf16), V(groups, rows, cols, dtype=bf16),
         V(groups, rows, cols, dtype=bf16), V(groups, rows, cols, dtype=bf16),
         V(tokens, cols, dtype=bf16), V(3, tokens, cols, dtype=bf16), V(tokens, cols),
-        V(groups, 2, rows, cols, dtype=bf16), V(groups, 2, rows, cols, dtype=bf16),
-        dma((4,)), dma((4,)), dma((6,)), dma((6,)),
+        V(groups, rows, cols, dtype=bf16), V(groups, rows, cols, dtype=bf16),
+        V(groups, rows, cols, dtype=bf16), V(groups, rows, cols, dtype=bf16),
+        dma((9,)), dma((5,)), dma((5,)), dma((8,)), dma((8,)),
     ]
     out = jax.ShapeDtypeStruct(pair.shape, bf16)
     return pl.pallas_call(
         kernel,
         out_shape=(out, out),
-        in_specs=[vm, sm, vm, vm, vm, vm, vm, vm, vm, vm],
+        in_specs=[hbm] * 9,
         out_specs=(vm, vm),
         scratch_shapes=scratch,
         compiler_params=pltpu.CompilerParams(
-            collective_id=0, has_side_effects=True, vmem_limit_bytes=32 << 20
+            collective_id=0, has_side_effects=True, vmem_limit_bytes=56 << 20
         ),
     )(
-        pair, token_mask, token_mask.reshape(tokens // cols, cols), norm_gain.reshape(1, feat),
+        pair, token_mask.reshape(tokens // cols, cols), norm_gain.reshape(1, feat),
         w_a, w_b, w_gate, hid_gain.reshape(1, hid), w_out, cotangent,
     )
 

time: 71 us -> 65.5 us (0.923)
  the two profiles are of different devices: /device:TPU:2 before, /device:TPU:7 now
where the time goes in v3:
time: 65.5 us; the launch traced here: 65.4 us
  Pallas kernels  62.3 us (95%)
  local copies, waits for them, and re-layouts  2.42 us (4%)
    pallas_call x1, Pallas kernels, local(): pl.pallas_call(kernel, out_shape=(out, out), in_specs=[hbm] * 9, out_spec...  62.3 us
    unnamed x4, local copies, waits for them, and re-layouts  2.42 us

profile of v3, /device:TPU:7, one launch (start us, length us, event | category | flops | bytes accessed | tf_op | source)
XLA Modules:
  0.0 65.4 jit_solution(4211849933053721997)
XLA Ops:
  0.6 62.3 %shard_map.104 = (bf16[8,128,128]{2,1,0:T(8,128)(2,1)}, bf16[8,128,128]{2,1,0:T(8,128)(2,1)}) custom-call(bf16[8,128,128]{2,1,0:T(8,128)(2,1)} %pair_h.1, s32[4,128]{1,0:T(4,128)} %bitcast.3, f32[1,128]{1,0:T(1,128)} %bitcast.4, bf16[128,128]{1,0:T(8,128)(2,1)} %wa_h.1, bf16[128,128]{1,0:T(8,128)(2,1)} %wb_h.1, bf16[128,128]{1,0:T(8,128)(2,1)} %wg_h.1, ...), custom_call_target="tpu_custom_call" | custom-call | tf_op jit(solution)/shard_map/pallas_call | solution.py:330
  63.0 0.0 copy-start
  63.0 1.7 %copy.13 = bf16[8,128,128]{2,1,0:T(8,128)(2,1)} copy(bf16[8,128,128]{2,1,0:T(8,128)(2,1)} %get-tuple-element.4) | data formatting | bytes 524288
  64.7 0.0 copy-done
  64.7 0.7 %copy.14 = bf16[8,128,128]{2,1,0:T(8,128)(2,1)} copy(bf16[8,128,128]{2,1,0:T(8,128)(2,1)S(1)} %copy-done) | data formatting | bytes 524288
Async XLA Ops:
  63.0 1.7 %copy-start = (bf16[8,128,128]{2,1,0:T(8,128)(2,1)S(1)}, bf16[8,128,128]{2,1,0:T(8,128)(2,1)}, u32[]{:S(2)}) copy-start(bf16[8,128,128]{2,1,0:T(8,128)(2,1)} %get-tuple-element.5) | copy-start | bytes 786436

commit v4 on v3

v4 whole, which is shorter than its diff:
```python
import jax
import jax.numpy as jnp
from jax import lax
from jax.experimental import pallas as pl
from jax.experimental.pallas import tpu as pltpu
from jax.sharding import PartitionSpec as P

epsilon = 1e-05
MESH = pl.DeviceIdType.MESH
f32 = jnp.float32
bf16 = jnp.bfloat16


def mean0(values):
    return jnp.sum(values, axis=0, keepdims=True) * (1.0 / values.shape[0])


def mm(a, b):
    return jnp.dot(a, b, preferred_element_type=f32)


def column(row):
    n = row.shape[1]
    same = lax.broadcasted_iota(jnp.int32, (n, n), 0) == lax.broadcasted_iota(jnp.int32, (n, n), 1)
    return jnp.sum(jnp.where(same, row, 0.0), axis=1, keepdims=True)


def kernel(
    pair_h, mask_h, ngain_h, wa_h, wb_h, wg_h, hgain_h, wo_h, cot_h,
    upd, pgrad,
    pair, mask, ngain, wa, wb, wg, hgain, wo, cot, pmask,
    wabt, wgt, wot, ng, hg,
    normed, pinv, zn, proj, gate, cgate, qs, mq, xn, gz,
    st_a, st_b, left, right, left_t,
    s1, r1, x1s, x1r, x1n, x1m, own, s2, r2, s3, r3, x2, gr, s4a, s4b, r4a, r4b,
    sem_i, sem_s, sem_r, sem_xs, sem_xr,
):
    rows, cols, feat = pair.shape
    hid = wo.shape[0]
    groups = hid
    tokens = rows * groups
    me = lax.axis_index("row")
    ch = lax.axis_index("chan")
    sib = ch + 1 - 2 * lax.rem(ch, 2)
    nei = lax.rem(ch + 2, 4)
    diag = lax.rem(sib + 2, 4)

    def fetch(i):
        src = (pair_h, wa_h, wb_h, ngain_h, mask_h, wg_h, wo_h, hgain_h, cot_h)[i]
        dst = (pair, wa, wb, ngain, mask, wg, wo, hgain, cot)[i]
        return pltpu.make_async_copy(src, dst, sem_i.at[i])

    for i in range(9):
        fetch(i).start()

    planes = 4
    size = groups // planes
    offsets = (2, 1, 3, 0)
    my_y, my_x, my_z = me // 16, me // 8 % 2, me % 8

    def plane(d):
        return (my_y + offsets[d]) % planes

    def source_plane(d):
        return (my_y + planes - offsets[d]) % planes

    def target(d, u):
        iz, ix = u % 8, u // 8
        dz = 4 + (iz + 1) // 2 * (1 - 2 * (iz % 2))
        return plane(d) * size + (my_x + 1 - ix) % 2 * 8 + (my_z + dz) % 8

    def count(d):
        return size if offsets[d] else size - 1

    barrier = pltpu.get_barrier_semaphore()

    for d in range(planes):

        def greet(u, _):
            pl.semaphore_signal(
                barrier, inc=1, device_id=(target(d, u), ch), device_id_type=MESH
            )
            return 0

        lax.fori_loop(0, count(d), greet, 0)
    for t in (sib, nei):
        pl.semaphore_signal(barrier, inc=1, device_id=(me, t), device_id_type=MESH)

    def send_plane(src, dst, d, slot, arrival):
        def one(u, _):
            t = target(d, u)
            pltpu.make_async_remote_copy(
                src.at[t], dst.at[me], sem_s.at[slot], sem_r.at[arrival],
                device_id=(t, ch), device_id_type=MESH,
            ).start()
            return 0

        lax.fori_loop(0, count(d), one, 0)
        if not offsets[d]:
            dst[me] = src[me]

    def wait_blocks(buf, n, sem):
        some = buf.at[pl.ds(0, n)]
        pltpu.make_async_copy(some, some, sem).wait()

    def wait_all(buf, sem):
        wait_blocks(buf, groups - 1, sem)

    def swap(src, dst, to, slot):
        return pltpu.make_async_remote_copy(
            src, dst, sem_xs.at[slot], sem_xr.at[slot],
            device_id=(me, to), device_id_type=MESH,
        )

    for i in range(5):
        fetch(i).wait()
    wa_f, wb_f = wa[...].astype(f32), wb[...].astype(f32)
    wabt[0:feat, :] = wa_f.T.astype(bf16)
    wabt[feat : 2 * feat, :] = wb_f.T.astype(bf16)
    ng[...] = jnp.broadcast_to(column(ngain[...]), (feat, cols))
    place = lax.broadcasted_iota(jnp.int32, (rows, cols), 1)
    step = lax.broadcasted_iota(jnp.int32, (rows, cols), 0)
    near = mask[pl.ds(me * rows // cols, 1), :].astype(f32)
    mask_rows = jnp.sum(
        jnp.where(place == step + me * rows % cols, near, 0.0), axis=1, keepdims=True
    )
    pmask[...] = mask_rows * mask[pl.ds(ch, 1), :].astype(f32)

    def forward(r, _):
        x = pair[r].astype(f32).T
        centered = x - mean0(x)
        inv = lax.rsqrt(mean0(centered * centered) + epsilon)
        n = centered * inv
        normed[r] = n
        pinv[r] = inv
        z = (n * ng[...]).astype(bf16)
        zn[r] = z
        p = mm(wabt[...], z)
        m = pmask[pl.ds(r, 1), :]
        sa = jax.nn.sigmoid(p[0:hid])
        sb = jax.nn.sigmoid(p[2 * hid : 3 * hid])
        ma, mb = sa * m, sb * m
        va, vb = p[hid : 2 * hid], p[3 * hid : 4 * hid]
        la, lb = ma * va, mb * vb
        st_a[pl.ds(r, hid, stride=rows), :] = la
        st_b[pl.ds(r, hid, stride=rows), :] = lb
        proj[r, 0:hid] = la * (1.0 - sa)
        proj[r, hid : 2 * hid] = ma
        proj[r, 2 * hid : 3 * hid] = lb * (1.0 - sb)
        proj[r, 3 * hid : 4 * hid] = mb
        return 0

    lax.fori_loop(0, rows, forward, 0)
    s1[:, 0] = st_a[...].reshape(groups, rows, cols).astype(bf16)
    s1[:, 1] = st_b[...].reshape(groups, rows, cols).astype(bf16)
    pl.semaphore_wait(barrier, groups - 1 + 2)
    for d in range(planes):
        send_plane(s1, r1, d, 0, 0)

    for i in range(5, 9):
        fetch(i).wait()
    hg[...] = jnp.broadcast_to(column(hgain[...]), (hid, cols))
    wgt[...] = wg[...].astype(f32).T.astype(bf16)
    wot[...] = wo[...].astype(f32).T.astype(bf16)

    def gates(r, _):
        g = jax.nn.sigmoid(mm(wgt[...], zn[r]))
        gate[r] = g
        u = cot[r].astype(f32).T * g
        cgate[r] = u * (1.0 - g)
        q = mm(wo[...], u.astype(bf16)) * hg[...]
        qs[r] = q
        mq[r] = mean0(q)
        return 0

    lax.fori_loop(0, rows, gates, 0)

    wait_all(r1, sem_r.at[0])
    left[...] = r1[:, 0].astype(f32).reshape(tokens, cols).astype(bf16)
    right[...] = r1[:, 1].astype(f32).reshape(tokens, cols).astype(bf16)

    block = tokens // planes

    def rows_of(p):
        return pl.ds(pl.multiple_of(p * block, block), block)

    def part(p, t):
        return lax.dot_general(
            left[rows_of(p), :], right[rows_of(t), :], (((1,), (1,)), ((), ())),
            preferred_element_type=f32,
        )

    def pair_up(d):
        return swap(x1s.at[d], x1r.at[d], sib, d)

    def hand_over(d):
        return swap(x1n.at[d], x1m.at[d], nei, planes + d)

    for d in range(planes):
        x1s[d, 0] = part(plane(d), diag).astype(bf16)
        x1s[d, 1] = part(plane(d), sib).astype(bf16)
        pair_up(d).start()
    for d in range(planes):
        mine = part(plane(d), nei)
        pair_up(d).wait_recv()
        x1n[d] = (mine + x1r[d, 0].astype(f32)).astype(bf16)
        hand_over(d).start()
    for d in range(planes):
        own[d] = part(plane(d), ch) + x1r[d, 1].astype(f32)
    for d in range(planes):
        hand_over(d).wait_recv()
        tri = own[d] + x1m[d].astype(f32)
        s2[pl.ds(plane(d) * size, size)] = tri.reshape(size, rows, cols).astype(bf16)
        send_plane(s2, r2, d, 1, 1)
    for p in range(planes):
        left_t[p] = left[p * block : (p + 1) * block, :].astype(f32).T.astype(bf16)

    wait_all(r2, sem_r.at[1])
    st_a[...] = r2[...].astype(f32).reshape(tokens, cols)

    def middle(r, _):
        t = st_a[pl.ds(r, hid, stride=rows), :]
        centered = t - mean0(t)
        inv = lax.rsqrt(mean0(centered * centered) + epsilon)
        n = centered * inv
        xn[r] = (n * hg[...]).astype(bf16)
        q = qs[r]
        grad = inv * (q - mq[r] - n * mean0(q * n))
        st_b[pl.ds(r, hid, stride=rows), :] = grad
        return 0

    lax.fori_loop(0, rows, middle, 0)
    s3[...] = st_b[...].reshape(groups, rows, cols).astype(bf16)
    for d in range(planes):
        send_plane(s3, r3, d, 2, 2 + d)

    def outputs(r, _):
        y = mm(wot[...], xn[r])
        upd[r] = (gate[r] * y).T.astype(bf16)
        gz[r] = mm(wg[...], (cgate[r] * y).astype(bf16))
        return 0

    lax.fori_loop(0, rows, outputs, 0)

    def at(c, p):
        return x2.at[c, p]

    def onward(d, p):
        return swap(at(ch, p), at(ch, p), nei, 8 + d)

    def beside(d, p):
        return swap(at(ch, p), at(ch, p), sib, 12 + d)

    def relay(d, p):
        return swap(at(nei, p), at(nei, p), sib, 16 + d)

    def take(d):
        p = source_plane(d)
        wait_blocks(r3, count(d), sem_r.at[2 + d])
        grad = r3[pl.ds(p * size, size)].astype(f32).reshape(block, cols)
        x2[ch, p] = grad.astype(bf16)
        onward(d, p).start()
        beside(d, p).start()

    def forward_on(d):
        p = source_plane(d)
        onward(d, p).wait_recv()
        relay(d, p).start()

    def left_grads(d):
        p = source_plane(d)
        beside(d, p).wait_recv()
        relay(d, p).wait_recv()
        total = mm(x2[0, p], right[0:block, :])
        for c in range(1, planes):
            total += mm(x2[c, p], right[c * block : (c + 1) * block, :])
        s4a[pl.ds(p * size, size)] = total.reshape(size, rows, cols).astype(bf16)

    def right_part(d, c):
        p = source_plane(d)
        return mm(left_t[p], x2[c, p])

    def work(d, first):
        left_grads(d)
        send_plane(s4a, r4a, (0, 2, 1, 3)[d], 3, 6)
        for c in range(planes):
            new = right_part(d, c)
            gr[c] = new if first else gr[c] + new

    for d in (3, 1, 2, 0):
        take(d)
    forward_on(3)
    forward_on(1)
    work(3, True)
    forward_on(2)
    work(1, False)
    forward_on(0)
    work(2, False)
    left_grads(0)
    send_plane(s4a, r4a, 0, 3, 6)
    for d in range(planes):
        c = plane(d)
        grad = (gr[c] + right_part(0, c)).T
        s4b[pl.ds(c * size, size)] = grad.reshape(size, rows, cols).astype(bf16)
        send_plane(s4b, r4b, d, 4, 7)

    wait_all(r4a, sem_r.at[6])
    st_a[...] = r4a[...].astype(f32).reshape(tokens, cols)

    def left_back(r, _):
        ga = st_a[pl.ds(r, hid, stride=rows), :]
        d = (proj[r, 0 : 2 * hid] * jnp.concatenate([ga, ga], axis=0)).astype(bf16)
        gz[r] += mm(wa[...], d)
        return 0

    lax.fori_loop(0, rows, left_back, 0)
    wait_all(r4b, sem_r.at[7])
    st_b[...] = r4b[...].astype(f32).reshape(tokens, cols)

    def backward(r, _):
        gb = st_b[pl.ds(r, hid, stride=rows), :]
        d = (proj[r, 2 * hid : 4 * hid] * jnp.concatenate([gb, gb], axis=0)).astype(bf16)
        q = (gz[r] + mm(wb[...], d)) * ng[...]
        n = normed[r]
        out = pinv[r] * (q - mean0(q) - n * mean0(q * n))
        pgrad[r] = out.T.astype(bf16)
        return 0

    lax.fori_loop(0, rows, backward, 0)

    for slot, buf in enumerate((s1, s2, s3, s4a, s4b)):
        wait_all(buf, sem_s.at[slot])
    for d in range(planes):
        p = source_plane(d)
        pair_up(d).wait_send()
        hand_over(d).wait_send()
        onward(d, p).wait_send()
        beside(d, p).wait_send()
        relay(d, p).wait_send()


def local(pair, token_mask, norm_gain, w_a, w_b, w_gate, hid_gain, w_out, cotangent):
    rows, cols, feat = pair.shape
    hid = w_out.shape[0]
    tokens = token_mask.shape[0]
    groups = tokens // rows
    vm = pl.BlockSpec(memory_space=pltpu.VMEM)
    hbm = pl.BlockSpec(memory_space=pl.ANY)
    dma = pltpu.SemaphoreType.DMA

    def V(*shape, dtype=f32):
        return pltpu.VMEM(shape, dtype)

    scratch = [
        V(rows, cols, feat, dtype=bf16), V(tokens // cols, cols, dtype=jnp.int32), V(1, feat),
        V(feat, 2 * hid, dtype=bf16), V(feat, 2 * hid, dtype=bf16), V(feat, feat, dtype=bf16),
        V(1, hid), V(hid, feat, dtype=bf16), V(rows, cols, feat, dtype=bf16), V(rows, cols),
        V(4 * hid, feat, dtype=bf16), V(feat, feat, dtype=bf16), V(feat, hid, dtype=bf16),
        V(feat, cols), V(hid, cols),
        V(rows, feat, cols), V(rows, 1, cols), V(rows, feat, cols, dtype=bf16),
        V(rows, 4 * hid, cols), V(rows, feat, cols), V(rows, feat, cols),
        V(rows, hid, cols), V(rows, 1, cols), V(rows, hid, cols, dtype=bf16),
        V(rows, feat, cols),
        V(tokens, cols), V(tokens, cols),
        V(tokens, cols, dtype=bf16), V(tokens, cols, dtype=bf16), V(4, cols, cols, dtype=bf16),
        V(groups, 2, rows, cols, dtype=bf16), V(groups, 2, rows, cols, dtype=bf16),
        V(4, 2, cols, cols, dtype=bf16), V(4, 2, cols, cols, dtype=bf16),
        V(4, cols, cols, dtype=bf16), V(4, cols, cols, dtype=bf16), V(4, cols, cols),
        V(groups, rows, cols, dtype=bf16), V(groups, rows, cols, dtype=bf16),
        V(groups, rows, cols, dtype=bf16), V(groups, rows, cols, dtype=bf16),
        V(4, 4, cols, cols, dtype=bf16), V(4, cols, cols),
        V(groups, rows, cols, dtype=bf16), V(groups, rows, cols, dtype=bf16),
        V(groups, rows, cols, dtype=bf16), V(groups, rows, cols, dtype=bf16),
        dma((9,)), dma((5,)), dma((8,)), dma((20,)), dma((20,)),
    ]
    out = jax.ShapeDtypeStruct(pair.shape, bf16)
    return pl.pallas_call(
        kernel,
        out_shape=(out, out),
        in_specs=[hbm] * 9,
        out_specs=(vm, vm),
        scratch_shapes=scratch,
        compiler_params=pltpu.CompilerParams(
            collective_id=0, has_side_effects=True, vmem_limit_bytes=56 << 20
        ),
    )(
        pair, token_mask.reshape(tokens // cols, cols), norm_gain.reshape(1, feat),
        w_a, w_b, w_gate, hid_gain.reshape(1, hid), w_out, cotangent,
    )


def solution(mesh):
    in_specs = (P("row", "chan", None), P(), P(), P(), P(), P(), P(), P(), P("row", "chan", None))
    out_specs = (P("row", "chan", None), P("row", "chan", None))
    return jax.shard_map(local, mesh=mesh, in_specs=in_specs, out_specs=out_specs, check_vma=False)
```

time: 65.5 us -> 65 us (level)
  the two profiles are of different devices: /device:TPU:7 before, /device:TPU:1 now
where the time goes in v4:
time: 65 us; the launch traced here: 64.9 us
  Pallas kernels  61.8 us (95%)
  local copies, waits for them, and re-layouts  2.42 us (4%)
  between operations  0.65 us (1%)
    pallas_call x1, Pallas kernels, local(): pl.pallas_call(kernel, out_shape=(out, out), in_specs=[hbm] * 9, out_spec...  61.8 us
    unnamed x4, local copies, waits for them, and re-layouts  2.42 us

profile of v4, /device:TPU:1, one launch (start us, length us, event | category | flops | bytes accessed | tf_op | source)
XLA Modules:
  0.0 64.9 jit_solution(6236778679390045349)
XLA Ops:
  0.6 61.8 %shard_map.104 = (bf16[8,128,128]{2,1,0:T(8,128)(2,1)}, bf16[8,128,128]{2,1,0:T(8,128)(2,1)}) custom-call(bf16[8,128,128]{2,1,0:T(8,128)(2,1)} %pair_h.1, s32[4,128]{1,0:T(4,128)} %bitcast.3, f32[1,128]{1,0:T(1,128)} %bitcast.4, bf16[128,128]{1,0:T(8,128)(2,1)} %wa_h.1, bf16[128,128]{1,0:T(8,128)(2,1)} %wb_h.1, bf16[128,128]{1,0:T(8,128)(2,1)} %wg_h.1, ...), custom_call_target="tpu_custom_call" | custom-call | tf_op jit(solution)/shard_map/pallas_call | solution.py:377
  62.5 0.0 copy-start
  62.5 1.7 %copy.13 = bf16[8,128,128]{2,1,0:T(8,128)(2,1)} copy(bf16[8,128,128]{2,1,0:T(8,128)(2,1)} %get-tuple-element.4) | data formatting | bytes 524288
  64.2 0.0 copy-done
  64.2 0.7 %copy.14 = bf16[8,128,128]{2,1,0:T(8,128)(2,1)} copy(bf16[8,128,128]{2,1,0:T(8,128)(2,1)S(1)} %copy-done) | data formatting | bytes 524288
Async XLA Ops:
  62.5 1.7 %copy-start = (bf16[8,128,128]{2,1,0:T(8,128)(2,1)S(1)}, bf16[8,128,128]{2,1,0:T(8,128)(2,1)}, u32[]{:S(2)}) copy-start(bf16[8,128,128]{2,1,0:T(8,128)(2,1)} %get-tuple-element.5) | copy-start | bytes 786436

commit v5 on v4

--- a/solution.py
+++ b/solution.py
@@ -27,13 +27,13 @@
 
 def kernel(
     pair_h, mask_h, ngain_h, wa_h, wb_h, wg_h, hgain_h, wo_h, cot_h,
-    upd, pgrad,
-    pair, mask, ngain, wa, wb, wg, hgain, wo, cot, pmask,
+    upd_h, pgrad_h,
+    upd, pgrad, pair, mask, ngain, wa, wb, wg, hgain, wo, cot, pmask,
     wabt, wgt, wot, ng, hg,
     normed, pinv, zn, proj, gate, cgate, qs, mq, xn, gz,
     st_a, st_b, left, right, left_t,
-    s1, r1, x1s, x1r, x1n, x1m, own, s2, r2, s3, r3, x2, gr, s4a, s4b, r4a, r4b,
-    sem_i, sem_s, sem_r, sem_xs, sem_xr,
+    s1, r1, x1s, x1r, own, s2, s2n, r2, r2n, s3, r3, r3n, g, gs, gr, s4a, s4b, r4a, r4b,
+    sem_i, sem_o, sem_s, sem_r, sem_xs, sem_xr,
 ):
     rows, cols, feat = pair.shape
     hid = wo.shape[0]
@@ -97,6 +97,28 @@
 
         lax.fori_loop(0, count(d), one, 0)
         if not offsets[d]:
+            dst[me] = src[me]
+
+    def send_both(src, dst, slot, arrival, src_n, dst_n, slot_n, arrival_n, d):
+        def over(u):
+            t = target(d, u)
+            pltpu.make_async_remote_copy(
+                src_n.at[t], dst_n.at[me], sem_s.at[slot_n], sem_r.at[arrival_n],
+                device_id=(t, nei), device_id_type=MESH,
+            ).start()
+            return t
+
+        def one(u, _):
+            t = over(u)
+            pltpu.make_async_remote_copy(
+                src.at[t], dst.at[me], sem_s.at[slot], sem_r.at[arrival],
+                device_id=(t, ch), device_id_type=MESH,
+            ).start()
+            return 0
+
+        lax.fori_loop(0, count(d), one, 0)
+        if not offsets[d]:
+            over(size - 1)
             dst[me] = src[me]
 
     def wait_blocks(buf, n, sem):
@@ -193,30 +215,26 @@
     def pair_up(d):
         return swap(x1s.at[d], x1r.at[d], sib, d)
 
-    def hand_over(d):
-        return swap(x1n.at[d], x1m.at[d], nei, planes + d)
-
-    for d in range(planes):
-        x1s[d, 0] = part(plane(d), diag).astype(bf16)
-        x1s[d, 1] = part(plane(d), sib).astype(bf16)
+    for d in range(planes):
+        x1s[d, 0] = part(plane(d), sib).astype(bf16)
+        x1s[d, 1] = part(plane(d), diag).astype(bf16)
         pair_up(d).start()
     for d in range(planes):
-        mine = part(plane(d), nei)
+        own[d, 0] = part(plane(d), ch)
+        own[d, 1] = part(plane(d), nei)
+    for d in range(planes):
         pair_up(d).wait_recv()
-        x1n[d] = (mine + x1r[d, 0].astype(f32)).astype(bf16)
-        hand_over(d).start()
-    for d in range(planes):
-        own[d] = part(plane(d), ch) + x1r[d, 1].astype(f32)
-    for d in range(planes):
-        hand_over(d).wait_recv()
-        tri = own[d] + x1m[d].astype(f32)
-        s2[pl.ds(plane(d) * size, size)] = tri.reshape(size, rows, cols).astype(bf16)
-        send_plane(s2, r2, d, 1, 1)
+        tri = own[d] + x1r[d].astype(f32)
+        at = pl.ds(plane(d) * size, size)
+        s2[at] = tri[0].reshape(size, rows, cols).astype(bf16)
+        s2n[at] = tri[1].reshape(size, rows, cols).astype(bf16)
+        send_both(s2, r2, 1, 1, s2n, r2n, 2, 2, d)
     for p in range(planes):
         left_t[p] = left[p * block : (p + 1) * block, :].astype(f32).T.astype(bf16)
 
     wait_all(r2, sem_r.at[1])
-    st_a[...] = r2[...].astype(f32).reshape(tokens, cols)
+    wait_blocks(r2n, groups, sem_r.at[2])
+    st_a[...] = (r2[...].astype(f32) + r2n[...].astype(f32)).reshape(tokens, cols)
 
     def middle(r, _):
         t = st_a[pl.ds(r, hid, stride=rows), :]
@@ -232,7 +250,7 @@
     lax.fori_loop(0, rows, middle, 0)
     s3[...] = st_b[...].reshape(groups, rows, cols).astype(bf16)
     for d in range(planes):
-        send_plane(s3, r3, d, 2, 2 + d)
+        send_both(s3, r3, 3, 3 + d, s3, r3n, 4, 7 + d, d)
 
     def outputs(r, _):
         y = mm(wot[...], xn[r])
@@ -241,70 +259,49 @@
         return 0
 
     lax.fori_loop(0, rows, outputs, 0)
-
-    def at(c, p):
-        return x2.at[c, p]
-
-    def onward(d, p):
-        return swap(at(ch, p), at(ch, p), nei, 8 + d)
+    pltpu.make_async_copy(upd, upd_h, sem_o.at[0]).start()
 
     def beside(d, p):
-        return swap(at(ch, p), at(ch, p), sib, 12 + d)
-
-    def relay(d, p):
-        return swap(at(nei, p), at(nei, p), sib, 16 + d)
+        return swap(g.at[p], gs.at[p], sib, planes + d)
 
     def take(d):
         p = source_plane(d)
-        wait_blocks(r3, count(d), sem_r.at[2 + d])
-        grad = r3[pl.ds(p * size, size)].astype(f32).reshape(block, cols)
-        x2[ch, p] = grad.astype(bf16)
-        onward(d, p).start()
+        at = pl.ds(p * size, size)
+        wait_blocks(r3, count(d), sem_r.at[3 + d])
+        wait_blocks(r3n, size, sem_r.at[7 + d])
+        g[p, 0] = r3[at].astype(f32).reshape(block, cols).astype(bf16)
+        g[p, 1] = r3n[at].astype(f32).reshape(block, cols).astype(bf16)
         beside(d, p).start()
 
-    def forward_on(d):
+    def work(d, first):
         p = source_plane(d)
-        onward(d, p).wait_recv()
-        relay(d, p).start()
-
-    def left_grads(d):
-        p = source_plane(d)
+        blocks = ((ch, g, 0), (nei, g, 1), (sib, gs, 0), (diag, gs, 1))
+        here = mm(g[p, 0], right[rows_of(ch), :]) + mm(g[p, 1], right[rows_of(nei), :])
+        for c, buf, i in blocks[:2]:
+            new = mm(left_t[p], buf[p, i])
+            gr[c] = new if first else gr[c] + new
         beside(d, p).wait_recv()
-        relay(d, p).wait_recv()
-        total = mm(x2[0, p], right[0:block, :])
-        for c in range(1, planes):
-            total += mm(x2[c, p], right[c * block : (c + 1) * block, :])
-        s4a[pl.ds(p * size, size)] = total.reshape(size, rows, cols).astype(bf16)
-
-    def right_part(d, c):
-        p = source_plane(d)
-        return mm(left_t[p], x2[c, p])
-
-    def work(d, first):
-        left_grads(d)
-        send_plane(s4a, r4a, (0, 2, 1, 3)[d], 3, 6)
-        for c in range(planes):
-            new = right_part(d, c)
+        there = mm(gs[p, 0], right[rows_of(sib), :]) + mm(gs[p, 1], right[rows_of(diag), :])
+        s4a[pl.ds(p * size, size)] = (here + there).reshape(size, rows, cols).astype(bf16)
+        send_plane(s4a, r4a, (0, 2, 1, 3)[d], 5, 11)
+        for c, buf, i in blocks[2:]:
+            new = mm(left_t[p], buf[p, i])
             gr[c] = new if first else gr[c] + new
 
-    for d in (3, 1, 2, 0):
-        take(d)
-    forward_on(3)
-    forward_on(1)
+    take(3)
+    take(1)
     work(3, True)
-    forward_on(2)
+    take(2)
     work(1, False)
-    forward_on(0)
+    take(0)
     work(2, False)
-    left_grads(0)
-    send_plane(s4a, r4a, 0, 3, 6)
+    work(0, False)
     for d in range(planes):
         c = plane(d)
-        grad = (gr[c] + right_part(0, c)).T
-        s4b[pl.ds(c * size, size)] = grad.reshape(size, rows, cols).astype(bf16)
-        send_plane(s4b, r4b, d, 4, 7)
-
-    wait_all(r4a, sem_r.at[6])
+        s4b[pl.ds(c * size, size)] = gr[c].T.reshape(size, rows, cols).astype(bf16)
+        send_plane(s4b, r4b, d, 6, 12)
+
+    wait_all(r4a, sem_r.at[11])
     st_a[...] = r4a[...].astype(f32).reshape(tokens, cols)
 
     def left_back(r, _):
@@ -314,7 +311,7 @@
         return 0
 
     lax.fori_loop(0, rows, left_back, 0)
-    wait_all(r4b, sem_r.at[7])
+    wait_all(r4b, sem_r.at[12])
     st_b[...] = r4b[...].astype(f32).reshape(tokens, cols)
 
     def backward(r, _):
@@ -324,19 +321,29 @@
         n = normed[r]
         out = pinv[r] * (q - mean0(q) - n * mean0(q * n))
         pgrad[r] = out.T.astype(bf16)
+        pltpu.make_async_copy(pgrad.at[r], pgrad_h.at[r], sem_o.at[1]).start()
         return 0
 
     lax.fori_loop(0, rows, backward, 0)
 
-    for slot, buf in enumerate((s1, s2, s3, s4a, s4b)):
+    for slot, buf in ((0, s1), (1, s2), (3, s3), (5, s4a), (6, s4b)):
         wait_all(buf, sem_s.at[slot])
-    for d in range(planes):
-        p = source_plane(d)
+    for slot, buf in ((2, s2n), (4, s3)):
+        wait_blocks(buf, groups, sem_s.at[slot])
+    for d in range(planes):
         pair_up(d).wait_send()
-        hand_over(d).wait_send()
-        onward(d, p).wait_send()
-        beside(d, p).wait_send()
-        relay(d, p).wait_send()
+        beside(d, source_plane(d)).wait_send()
+    pltpu.make_async_copy(upd, upd_h, sem_o.at[0]).wait()
+    pltpu.make_async_copy(pgrad, pgrad_h, sem_o.at[1]).wait()
+
+
+def hand_out(a, b, a_out, b_out, sem):
+    first = pltpu.make_async_copy(a, a_out, sem.at[0])
+    second = pltpu.make_async_copy(b, b_out, sem.at[1])
+    first.start()
+    second.start()
+    first.wait()
+    second.wait()
 
 
 def local(pair, token_mask, norm_gain, w_a, w_b, w_gate, hid_gain, w_out, cotangent):
@@ -344,7 +351,6 @@
     hid = w_out.shape[0]
     tokens = token_mask.shape[0]
     groups = tokens // rows
-    vm = pl.BlockSpec(memory_space=pltpu.VMEM)
     hbm = pl.BlockSpec(memory_space=pl.ANY)
     dma = pltpu.SemaphoreType.DMA
 
@@ -352,6 +358,7 @@
         return pltpu.VMEM(shape, dtype)
 
     scratch = [
+        V(rows, cols, feat, dtype=bf16), V(rows, cols, feat, dtype=bf16),
         V(rows, cols, feat, dtype=bf16), V(tokens // cols, cols, dtype=jnp.int32), V(1, feat),
         V(feat, 2 * hid, dtype=bf16), V(feat, 2 * hid, dtype=bf16), V(feat, feat, dtype=bf16),
         V(1, hid), V(hid, feat, dtype=bf16), V(rows, cols, feat, dtype=bf16), V(rows, cols),
@@ -364,21 +371,18 @@
         V(tokens, cols), V(tokens, cols),
         V(tokens, cols, dtype=bf16), V(tokens, cols, dtype=bf16), V(4, cols, cols, dtype=bf16),
         V(groups, 2, rows, cols, dtype=bf16), V(groups, 2, rows, cols, dtype=bf16),
-        V(4, 2, cols, cols, dtype=bf16), V(4, 2, cols, cols, dtype=bf16),
-        V(4, cols, cols, dtype=bf16), V(4, cols, cols, dtype=bf16), V(4, cols, cols),
-        V(groups, rows, cols, dtype=bf16), V(groups, rows, cols, dtype=bf16),
-        V(groups, rows, cols, dtype=bf16), V(groups, rows, cols, dtype=bf16),
-        V(4, 4, cols, cols, dtype=bf16), V(4, cols, cols),
-        V(groups, rows, cols, dtype=bf16), V(groups, rows, cols, dtype=bf16),
-        V(groups, rows, cols, dtype=bf16), V(groups, rows, cols, dtype=bf16),
-        dma((9,)), dma((5,)), dma((8,)), dma((20,)), dma((20,)),
+        V(4, 2, cols, cols, dtype=bf16), V(4, 2, cols, cols, dtype=bf16), V(4, 2, cols, cols),
+        *[V(groups, rows, cols, dtype=bf16) for _ in range(7)],
+        V(4, 2, cols, cols, dtype=bf16), V(4, 2, cols, cols, dtype=bf16), V(4, cols, cols),
+        *[V(groups, rows, cols, dtype=bf16) for _ in range(4)],
+        dma((9,)), dma((2,)), dma((7,)), dma((13,)), dma((8,)), dma((8,)),
     ]
     out = jax.ShapeDtypeStruct(pair.shape, bf16)
-    return pl.pallas_call(
+    results = pl.pallas_call(
         kernel,
         out_shape=(out, out),
         in_specs=[hbm] * 9,
-        out_specs=(vm, vm),
+        out_specs=(hbm, hbm),
         scratch_shapes=scratch,
         compiler_params=pltpu.CompilerParams(
             collective_id=0, has_side_effects=True, vmem_limit_bytes=56 << 20
@@ -387,6 +391,13 @@
         pair, token_mask.reshape(tokens // cols, cols), norm_gain.reshape(1, feat),
         w_a, w_b, w_gate, hid_gain.reshape(1, hid), w_out, cotangent,
     )
+    return pl.pallas_call(
+        hand_out,
+        out_shape=(out, out),
+        in_specs=[hbm, hbm],
+        out_specs=(hbm, hbm),
+        scratch_shapes=[dma((2,))],
+    )(*results)
 
 
 def solution(mesh):

time: 65 us -> 77.5 us (1.19)
  Pallas kernels: 61.8 us -> 76.7 us
  local copies, waits for them, and re-layouts: 2.42 us -> 0 us
    pallas_call x0 -> x1, Pallas kernels: none -> 17 us  [local(): pl.pallas_call(hand_out, out_shape=(out, out), in_specs=[hbm, hbm], out_s...]
    unnamed x4 -> x0, local copies, waits for them, and re-layouts: 2.42 us -> none
    pallas_call x1, Pallas kernels: 61.8 us -> 59.7 us  [local(): pl.pallas_call(kernel, out_shape=(out, out), in_specs=[hbm] * 9, out_spec...]
where the time goes in v5:
time: 77.5 us; the launch traced here: 77.4 us
  Pallas kernels  76.7 us (99%)
    pallas_call x1, Pallas kernels, local(): pl.pallas_call(kernel, out_shape=(out, out), in_specs=[hbm] * 9, out_spec...  59.7 us
    pallas_call x1, Pallas kernels, local(): pl.pallas_call(hand_out, out_shape=(out, out), in_specs=[hbm, hbm], out_s...  17 us

profile of v5, /device:TPU:1, one launch (start us, length us, event | category | flops | bytes accessed | tf_op | source)
XLA Modules:
  0.0 77.4 jit_solution(14968471416058867665)
XLA Ops:
  0.6 59.7 %shard_map.104 = (bf16[8,128,128]{2,1,0:T(8,128)(2,1)}, bf16[8,128,128]{2,1,0:T(8,128)(2,1)}) custom-call(bf16[8,128,128]{2,1,0:T(8,128)(2,1)} %pair_h.1, s32[4,128]{1,0:T(4,128)} %bitcast.3, f32[1,128]{1,0:T(1,128)} %bitcast.4, bf16[128,128]{1,0:T(8,128)(2,1)} %wa_h.1, bf16[128,128]{1,0:T(8,128)(2,1)} %wb_h.1, bf16[128,128]{1,0:T(8,128)(2,1)} %wg_h.1, ...), custom_call_target="tpu_custom_call" | custom-call | tf_op jit(solution)/shard_map/pallas_call | solution.py:381
  60.4 17.0 %shard_map.105 = (bf16[8,128,128]{2,1,0:T(8,128)(2,1)}, bf16[8,128,128]{2,1,0:T(8,128)(2,1)}) custom-call(bf16[8,128,128]{2,1,0:T(8,128)(2,1)} %get-tuple-element.4.a, bf16[8,128,128]{2,1,0:T(8,128)(2,1)} %get-tuple-element.5.b), custom_call_target="tpu_custom_call" | custom-call | tf_op jit(solution)/shard_map/pallas_call | solution.py:394

commit v6 on v2

v6 whole, which is shorter than its diff:
```python
import jax
import jax.numpy as jnp
from jax import lax
from jax.experimental import pallas as pl
from jax.experimental.pallas import tpu as pltpu
from jax.sharding import PartitionSpec as P

epsilon = 1e-05
MESH = pl.DeviceIdType.MESH
f32 = jnp.float32
bf16 = jnp.bfloat16


def mean0(values):
    return jnp.sum(values, axis=0, keepdims=True) * (1.0 / values.shape[0])


def mm(a, b):
    return jnp.dot(a, b, preferred_element_type=f32)


def column(row):
    n = row.shape[1]
    same = lax.broadcasted_iota(jnp.int32, (n, n), 0) == lax.broadcasted_iota(jnp.int32, (n, n), 1)
    return jnp.sum(jnp.where(same, row, 0.0), axis=1, keepdims=True)


def kernel(
    pair_h, mask_h, ngain_h, wa_h, wb_h, wg_h, hgain_h, wo_h, cot_h,
    upd_h, pgrad_h,
    upd, pgrad, pair, mask, ngain, wa, wb, wg, hgain, wo, cot, pmask,
    wabt, wgt, wot, ng, hg,
    normed, pinv, zn, proj, gate, cgate, qs, mq, xn, gz,
    st_a, st_b,
    s1a, s1b, r1a, r1b, lf, rf, s2, r2, s3, r3, g, gt, gtt, gr, s4a, s4b, r4a, r4b,
    sem_i, sem_o, sem_s, sem_r, sem_xs, sem_xr,
):
    rows, cols, feat = pair.shape
    hid = wo.shape[0]
    groups = hid
    tokens = rows * groups
    me = lax.axis_index("row")
    ch = lax.axis_index("chan")
    sib = ch + 1 - 2 * lax.rem(ch, 2)
    nei = lax.rem(ch + 2, 4)
    diag = lax.rem(sib + 2, 4)

    def fetch(i):
        src = (pair_h, wa_h, wb_h, ngain_h, mask_h, wg_h, wo_h, hgain_h, cot_h)[i]
        dst = (pair, wa, wb, ngain, mask, wg, wo, hgain, cot)[i]
        return pltpu.make_async_copy(src, dst, sem_i.at[i])

    for i in range(9):
        fetch(i).start()

    planes = 4
    size = groups // planes
    block = tokens // planes
    offsets = (2, 1, 3, 0)
    my_y, my_x, my_z = me // size, me // 8 % 2, me % 8
    at_home = my_y == ch

    def within(u):
        iz, ix = u % 8, u // 8
        dz = 4 + (iz + 1) // 2 * (1 - 2 * (iz % 2))
        return (my_x + 1 - ix) % 2 * 8 + (my_z + dz) % 8

    barrier = pltpu.get_barrier_semaphore()

    def greet(u, _):
        for c in range(planes):
            pl.semaphore_signal(
                barrier, inc=1, device_id=(ch * size + within(u), c), device_id_type=MESH
            )
        return 0

    lax.fori_loop(0, size - 1, greet, 0)
    for c in range(planes):

        @pl.when((ch != my_y) | (ch != c))
        def _():
            pl.semaphore_signal(
                barrier, inc=1, device_id=(ch * size + me % size, c), device_id_type=MESH
            )

    for t in (sib, nei):
        pl.semaphore_signal(barrier, inc=1, device_id=(me, t), device_id_type=MESH)

    def post(src, dst, row, c, slot):
        pltpu.make_async_remote_copy(
            src, dst, sem_s.at[slot], sem_r.at[slot],
            device_id=(row, c), device_id_type=MESH,
        ).start()

    def send_out(src, dst, slot):
        place = dst.at[ch, me % size]
        for d in range(planes):

            def one(u, _):
                t = (my_y + offsets[d]) % planes * size + within(u)
                post(src.at[t], place, t, my_y, slot)
                return 0

            lax.fori_loop(0, size if offsets[d] else size - 1, one, 0)

        @pl.when(at_home)
        def _():
            pltpu.make_async_copy(src.at[me], place, sem_r.at[slot]).start()

        @pl.when(ch != my_y)
        def _():
            post(src.at[me], place, me, my_y, slot)

    def send_back(src, dst, c, slot):
        def one(u, _):
            w = within(u)
            post(src.at[c, w], dst.at[me], ch * size + w, c, slot)
            return 0

        lax.fori_loop(0, size - 1, one, 0)
        w = me % size
        stays = at_home & (ch == c)

        @pl.when(stays)
        def _():
            pltpu.make_async_copy(src.at[c, w], dst.at[me], sem_r.at[slot]).start()

        @pl.when(jnp.logical_not(stays))
        def _():
            post(src.at[c, w], dst.at[me], ch * size + w, c, slot)

    def wait_in(buf, slot):
        pltpu.make_async_copy(buf, buf, sem_r.at[slot]).wait()

    def swap(src, dst, to, slot):
        return pltpu.make_async_remote_copy(
            src, dst, sem_xs.at[slot], sem_xr.at[slot],
            device_id=(me, to), device_id_type=MESH,
        )

    for i in range(5):
        fetch(i).wait()
    wa_f, wb_f = wa[...].astype(f32), wb[...].astype(f32)
    wabt[0:feat, :] = wa_f.T.astype(bf16)
    wabt[feat : 2 * feat, :] = wb_f.T.astype(bf16)
    ng[...] = jnp.broadcast_to(column(ngain[...]), (feat, cols))
    place = lax.broadcasted_iota(jnp.int32, (rows, cols), 1)
    step = lax.broadcasted_iota(jnp.int32, (rows, cols), 0)
    near = mask[pl.ds(me * rows // cols, 1), :].astype(f32)
    mask_rows = jnp.sum(
        jnp.where(place == step + me * rows % cols, near, 0.0), axis=1, keepdims=True
    )
    pmask[...] = mask_rows * mask[pl.ds(ch, 1), :].astype(f32)

    def forward(r, _):
        x = pair[r].astype(f32).T
        centered = x - mean0(x)
        inv = lax.rsqrt(mean0(centered * centered) + epsilon)
        n = centered * inv
        normed[r] = n
        pinv[r] = inv
        z = (n * ng[...]).astype(bf16)
        zn[r] = z
        p = mm(wabt[...], z)
        m = pmask[pl.ds(r, 1), :]
        sa = jax.nn.sigmoid(p[0:hid])
        sb = jax.nn.sigmoid(p[2 * hid : 3 * hid])
        ma, mb = sa * m, sb * m
        va, vb = p[hid : 2 * hid], p[3 * hid : 4 * hid]
        la, lb = ma * va, mb * vb
        st_a[pl.ds(r, hid, stride=rows), :] = la
        st_b[pl.ds(r, hid, stride=rows), :] = lb
        proj[r, 0:hid] = la * (1.0 - sa)
        proj[r, hid : 2 * hid] = ma
        proj[r, 2 * hid : 3 * hid] = lb * (1.0 - sb)
        proj[r, 3 * hid : 4 * hid] = mb
        return 0

    lax.fori_loop(0, rows, forward, 0)
    s1b[...] = st_b[...].reshape(groups, rows, cols).astype(bf16)
    s1a[...] = st_a[...].reshape(groups, rows, cols).astype(bf16)
    pl.semaphore_wait(barrier, groups + 2 - at_home.astype(jnp.int32))
    send_out(s1b, r1b, 0)
    send_out(s1a, r1a, 1)

    for i in range(5, 9):
        fetch(i).wait()
    hg[...] = jnp.broadcast_to(column(hgain[...]), (hid, cols))
    wgt[...] = wg[...].astype(f32).T.astype(bf16)
    wot[...] = wo[...].astype(f32).T.astype(bf16)

    def gates(r, _):
        g = jax.nn.sigmoid(mm(wgt[...], zn[r]))
        gate[r] = g
        u = cot[r].astype(f32).T * g
        cgate[r] = u * (1.0 - g)
        q = mm(wo[...], u.astype(bf16)) * hg[...]
        qs[r] = q
        mq[r] = mean0(q)
        return 0

    lax.fori_loop(0, rows, gates, 0)

    def unpack(buf):
        return buf[...].astype(f32).reshape(planes, block, cols).astype(bf16)

    halves = (pl.ds(0, 2), pl.ds(2, 2))

    def beside(buf, slot):
        return swap(buf.at[ch], buf.at[ch], sib, slot)

    def onward(buf, k, slot):
        return swap(buf.at[ch, halves[k]], buf.at[ch, halves[k]], nei, slot + 1 + k)

    def relay(buf, k, slot):
        return swap(buf.at[nei, halves[k]], buf.at[nei, halves[k]], sib, slot + 3 + k)

    def spread(buf, slot):
        onward(buf, 0, slot).start()
        onward(buf, 1, slot).start()
        beside(buf, slot).start()

    def pass_on(buf, slot):
        for k in (0, 1):
            onward(buf, k, slot).wait_recv()
            relay(buf, k, slot).start()

    wait_in(r1b, 0)
    rf[ch] = unpack(r1b)
    spread(rf, 0)

    wait_in(r1a, 1)
    lf[ch] = unpack(r1a)

    def triangle(c):
        total = 0.0
        for k in range(planes):
            total += lax.dot_general(
                lf[ch, k], rf[c, k], (((1,), (1,)), ((), ())), preferred_element_type=f32
            )
        s2[c] = total.reshape(size, rows, cols).astype(bf16)
        send_back(s2, r2, c, 2)

    triangle(ch)
    pass_on(rf, 0)
    beside(rf, 0).wait_recv()
    triangle(sib)
    triangle(nei)
    relay(rf, 0, 0).wait_recv()
    relay(rf, 1, 0).wait_recv()
    triangle(diag)

    spread(lf, 5)
    pass_on(lf, 5)

    wait_in(r2, 2)
    st_a[...] = r2[...].astype(f32).reshape(tokens, cols)

    def middle(r, _):
        t = st_a[pl.ds(r, hid, stride=rows), :]
        centered = t - mean0(t)
        inv = lax.rsqrt(mean0(centered * centered) + epsilon)
        n = centered * inv
        xn[r] = (n * hg[...]).astype(bf16)
        q = qs[r]
        grad = inv * (q - mq[r] - n * mean0(q * n))
        st_b[pl.ds(r, hid, stride=rows), :] = grad
        return 0

    lax.fori_loop(0, rows, middle, 0)
    s3[...] = st_b[...].reshape(groups, rows, cols).astype(bf16)
    send_out(s3, r3, 3)

    def outputs(r, _):
        y = mm(wot[...], xn[r])
        upd[r] = (gate[r] * y).T.astype(bf16)
        gz[r] = mm(wg[...], (cgate[r] * y).astype(bf16))
        return 0

    lax.fori_loop(0, rows, outputs, 0)
    pltpu.make_async_copy(upd, upd_h, sem_o.at[0]).start()

    beside(lf, 5).wait_recv()
    relay(lf, 0, 5).wait_recv()
    relay(lf, 1, 5).wait_recv()

    def trade(w):
        t = (diag, nei, sib)[w]
        return swap(g.at[t], gt.at[ch], t, 10 + w)

    wait_in(r3, 3)
    g[...] = unpack(r3)
    for w in (0, 1, 2):
        trade(w).start()
    for c in range(planes):
        total = mm(g[0], rf[0, c])
        for k in range(1, planes):
            total += mm(g[k], rf[k, c])
        s4a[c] = total.reshape(size, rows, cols).astype(bf16)
        send_back(s4a, r4a, c, 4)

    gtt[...] = g[ch].astype(f32).T.astype(bf16)
    for c in range(planes):
        gr[c] = mm(gtt[...], lf[ch, c])
    for w in (2, 1, 0):
        t = (diag, nei, sib)[w]
        trade(w).wait_recv()
        gtt[...] = gt[t].astype(f32).T.astype(bf16)
        for c in range(planes):
            total = gr[c] + mm(gtt[...], lf[t, c])
            if w:
                gr[c] = total
            else:
                s4b[c] = total.reshape(size, rows, cols).astype(bf16)
                send_back(s4b, r4b, c, 5)

    wait_in(r4a, 4)
    st_a[...] = r4a[...].astype(f32).reshape(tokens, cols)

    def left_back(r, _):
        ga = st_a[pl.ds(r, hid, stride=rows), :]
        d = (proj[r, 0 : 2 * hid] * jnp.concatenate([ga, ga], axis=0)).astype(bf16)
        gz[r] += mm(wa[...], d)
        return 0

    lax.fori_loop(0, rows, left_back, 0)
    wait_in(r4b, 5)
    st_b[...] = r4b[...].astype(f32).reshape(tokens, cols)

    def backward(r, _):
        gb = st_b[pl.ds(r, hid, stride=rows), :]
        d = (proj[r, 2 * hid : 4 * hid] * jnp.concatenate([gb, gb], axis=0)).astype(bf16)
        q = (gz[r] + mm(wb[...], d)) * ng[...]
        n = normed[r]
        out = pinv[r] * (q - mean0(q) - n * mean0(q * n))
        pgrad[r] = out.T.astype(bf16)
        pltpu.make_async_copy(pgrad.at[r], pgrad_h.at[r], sem_o.at[1]).start()
        return 0

    lax.fori_loop(0, rows, backward, 0)

    for slot in range(6):

        @pl.when(at_home)
        def _():
            some = s3.at[pl.ds(0, groups - 1)]
            pltpu.make_async_copy(some, some, sem_s.at[slot]).wait()

        @pl.when(ch != my_y)
        def _():
            pltpu.make_async_copy(s3, s3, sem_s.at[slot]).wait()

    for buf, slot in ((rf, 0), (lf, 5)):
        beside(buf, slot).wait_send()
        for k in (0, 1):
            onward(buf, k, slot).wait_send()
            relay(buf, k, slot).wait_send()
    for w in (0, 1, 2):
        trade(w).wait_send()
    pltpu.make_async_copy(upd, upd_h, sem_o.at[0]).wait()
    pltpu.make_async_copy(pgrad, pgrad_h, sem_o.at[1]).wait()


def local(pair, token_mask, norm_gain, w_a, w_b, w_gate, hid_gain, w_out, cotangent):
    rows, cols, feat = pair.shape
    hid = w_out.shape[0]
    tokens = token_mask.shape[0]
    groups = tokens // rows
    hbm = pl.BlockSpec(memory_space=pl.ANY)
    dma = pltpu.SemaphoreType.DMA

    def V(*shape, dtype=f32):
        return pltpu.VMEM(shape, dtype)

    scratch = [
        V(rows, cols, feat, dtype=bf16), V(rows, cols, feat, dtype=bf16),
        V(rows, cols, feat, dtype=bf16), V(tokens // cols, cols, dtype=jnp.int32), V(1, feat),
        V(feat, 2 * hid, dtype=bf16), V(feat, 2 * hid, dtype=bf16), V(feat, feat, dtype=bf16),
        V(1, hid), V(hid, feat, dtype=bf16), V(rows, cols, feat, dtype=bf16), V(rows, cols),
        V(4 * hid, feat, dtype=bf16), V(feat, feat, dtype=bf16), V(feat, hid, dtype=bf16),
        V(feat, cols), V(hid, cols),
        V(rows, feat, cols), V(rows, 1, cols), V(rows, feat, cols, dtype=bf16),
        V(rows, 4 * hid, cols), V(rows, feat, cols), V(rows, feat, cols),
        V(rows, hid, cols), V(rows, 1, cols), V(rows, hid, cols, dtype=bf16),
        V(rows, feat, cols),
        V(tokens, cols), V(tokens, cols),
        V(groups, rows, cols, dtype=bf16), V(groups, rows, cols, dtype=bf16),
        V(4, groups // 4, rows, cols, dtype=bf16), V(4, groups // 4, rows, cols, dtype=bf16),
        V(4, 4, cols, cols, dtype=bf16), V(4, 4, cols, cols, dtype=bf16),
        V(4, groups // 4, rows, cols, dtype=bf16), V(groups, rows, cols, dtype=bf16),
        V(groups, rows, cols, dtype=bf16), V(4, groups // 4, rows, cols, dtype=bf16),
        V(4, cols, cols, dtype=bf16), V(4, cols, cols, dtype=bf16), V(cols, cols, dtype=bf16),
        V(4, cols, cols),
        V(4, groups // 4, rows, cols, dtype=bf16), V(4, groups // 4, rows, cols, dtype=bf16),
        V(groups, rows, cols, dtype=bf16), V(groups, rows, cols, dtype=bf16),
        dma((9,)), dma((2,)), dma((6,)), dma((6,)), dma((13,)), dma((13,)),
    ]
    out = jax.ShapeDtypeStruct(pair.shape, bf16)
    return pl.pallas_call(
        kernel,
        out_shape=(out, out),
        in_specs=[hbm] * 9,
        out_specs=(hbm, hbm),
        scratch_shapes=scratch,
        compiler_params=pltpu.CompilerParams(
            collective_id=0, has_side_effects=True, vmem_limit_bytes=56 << 20
        ),
    )(
        pair, token_mask.reshape(tokens // cols, cols), norm_gain.reshape(1, feat),
        w_a, w_b, w_gate, hid_gain.reshape(1, hid), w_out, cotangent,
    )


def solution(mesh):
    in_specs = (P("row", "chan", None), P(), P(), P(), P(), P(), P(), P(), P("row", "chan", None))
    out_specs = (P("row", "chan", None), P("row", "chan", None))
    return jax.shard_map(local, mesh=mesh, in_specs=in_specs, out_specs=out_specs, check_vma=False)
```

time: 71 us -> 59.7 us (0.84)
  the two profiles are of different devices: /device:TPU:2 before, /device:TPU:1 now
where the time goes in v6:
time: 59.7 us; the launch traced here: 59.5 us
  Pallas kernels  56.5 us (95%)
  local copies, waits for them, and re-layouts  2.42 us (4%)
  between operations  0.65 us (1%)
    pallas_call x1, Pallas kernels, local(): pl.pallas_call(kernel, out_shape=(out, out), in_specs=[hbm] * 9, out_spec...  56.5 us
    unnamed x4, local copies, waits for them, and re-layouts  2.42 us

profile of v6, /device:TPU:1, one launch (start us, length us, event | category | flops | bytes accessed | tf_op | source)
XLA Modules:
  0.0 59.5 jit_solution(6356336408510476228)
XLA Ops:
  0.6 56.5 %shard_map.104 = (bf16[8,128,128]{2,1,0:T(8,128)(2,1)}, bf16[8,128,128]{2,1,0:T(8,128)(2,1)}) custom-call(bf16[8,128,128]{2,1,0:T(8,128)(2,1)} %pair_h.1, s32[4,128]{1,0:T(4,128)} %bitcast.3, f32[1,128]{1,0:T(1,128)} %bitcast.4, bf16[128,128]{1,0:T(8,128)(2,1)} %wa_h.1, bf16[128,128]{1,0:T(8,128)(2,1)} %wb_h.1, bf16[128,128]{1,0:T(8,128)(2,1)} %wg_h.1, ...), custom_call_target="tpu_custom_call" | custom-call | tf_op jit(solution)/shard_map/pallas_call | solution.py:399
  57.1 0.0 copy-start
  57.1 1.7 %copy.13 = bf16[8,128,128]{2,1,0:T(8,128)(2,1)} copy(bf16[8,128,128]{2,1,0:T(8,128)(2,1)} %get-tuple-element.4) | data formatting | bytes 524288
  58.8 0.0 copy-done
  58.8 0.7 %copy.14 = bf16[8,128,128]{2,1,0:T(8,128)(2,1)} copy(bf16[8,128,128]{2,1,0:T(8,128)(2,1)S(1)} %copy-done) | data formatting | bytes 524288
Async XLA Ops:
  57.1 1.7 %copy-start = (bf16[8,128,128]{2,1,0:T(8,128)(2,1)S(1)}, bf16[8,128,128]{2,1,0:T(8,128)(2,1)}, u32[]{:S(2)}) copy-start(bf16[8,128,128]{2,1,0:T(8,128)(2,1)} %get-tuple-element.5) | copy-start | bytes 786436

commit v7 on v6

--- a/solution.py
+++ b/solution.py
@@ -41,9 +41,8 @@
     tokens = rows * groups
     me = lax.axis_index("row")
     ch = lax.axis_index("chan")
-    sib = ch + 1 - 2 * lax.rem(ch, 2)
-    nei = lax.rem(ch + 2, 4)
-    diag = lax.rem(sib + 2, 4)
+    sib = ch + 1 - 2 * (ch % 2)
+    chans = (ch, sib, (ch + 2) % 4, (sib + 2) % 4)
 
     def fetch(i):
         src = (pair_h, wa_h, wb_h, ngain_h, mask_h, wg_h, wo_h, hgain_h, cot_h)[i]
@@ -56,9 +55,10 @@
     planes = 4
     size = groups // planes
     block = tokens // planes
-    offsets = (2, 1, 3, 0)
     my_y, my_x, my_z = me // size, me // 8 % 2, me % 8
-    at_home = my_y == ch
+    place = me % size
+    mine = ch * size + place
+    ahead, behind, across = (my_y + 1) % planes, (my_y + 3) % planes, (my_y + 2) % planes
 
     def within(u):
         iz, ix = u % 8, u // 8
@@ -67,75 +67,68 @@
 
     barrier = pltpu.get_barrier_semaphore()
 
+    def signal(row, c):
+        pl.semaphore_signal(barrier, inc=1, device_id=(row, c), device_id_type=MESH)
+
     def greet(u, _):
         for c in range(planes):
-            pl.semaphore_signal(
-                barrier, inc=1, device_id=(ch * size + within(u), c), device_id_type=MESH
-            )
+            signal(my_y * size + within(u), c)
         return 0
 
     lax.fori_loop(0, size - 1, greet, 0)
-    for c in range(planes):
-
-        @pl.when((ch != my_y) | (ch != c))
-        def _():
-            pl.semaphore_signal(
-                barrier, inc=1, device_id=(ch * size + me % size, c), device_id_type=MESH
-            )
-
-    for t in (sib, nei):
-        pl.semaphore_signal(barrier, inc=1, device_id=(me, t), device_id_type=MESH)
-
-    def post(src, dst, row, c, slot):
+    for c in chans[1:]:
+        signal(me, c)
+    for y in (across, ahead, behind):
+        signal(y * size + place, ch)
+
+    def post(src, dst, w, c, slot):
         pltpu.make_async_remote_copy(
             src, dst, sem_s.at[slot], sem_r.at[slot],
-            device_id=(row, c), device_id_type=MESH,
+            device_id=(my_y * size + w, c), device_id_type=MESH,
         ).start()
 
+    def keep(src, dst, slot):
+        pltpu.make_async_copy(src, dst, sem_r.at[slot]).start()
+
     def send_out(src, dst, slot):
-        place = dst.at[ch, me % size]
-        for d in range(planes):
-
-            def one(u, _):
-                t = (my_y + offsets[d]) % planes * size + within(u)
-                post(src.at[t], place, t, my_y, slot)
-                return 0
-
-            lax.fori_loop(0, size if offsets[d] else size - 1, one, 0)
-
-        @pl.when(at_home)
-        def _():
-            pltpu.make_async_copy(src.at[me], place, sem_r.at[slot]).start()
-
-        @pl.when(ch != my_y)
-        def _():
-            post(src.at[me], place, me, my_y, slot)
-
-    def send_back(src, dst, c, slot):
+        to = dst.at[ch, place]
+
         def one(u, _):
             w = within(u)
-            post(src.at[c, w], dst.at[me], ch * size + w, c, slot)
+            for c in chans:
+                post(src.at[c * size + w], to, w, c, slot)
             return 0
 
         lax.fori_loop(0, size - 1, one, 0)
-        w = me % size
-        stays = at_home & (ch == c)
-
-        @pl.when(stays)
+        for c in chans[1:]:
+            post(src.at[c * size + place], to, place, c, slot)
+        keep(src.at[mine], to, slot)
+
+    def send_back(src, dst, c, slot):
+        to = dst.at[mine]
+
+        def one(u, _):
+            w = within(u)
+            post(src.at[c, w], to, w, c, slot)
+            return 0
+
+        lax.fori_loop(0, size - 1, one, 0)
+
+        @pl.when(c == ch)
         def _():
-            pltpu.make_async_copy(src.at[c, w], dst.at[me], sem_r.at[slot]).start()
-
-        @pl.when(jnp.logical_not(stays))
+            keep(src.at[c, place], to, slot)
+
+        @pl.when(c != ch)
         def _():
-            post(src.at[c, w], dst.at[me], ch * size + w, c, slot)
+            post(src.at[c, place], to, place, c, slot)
 
     def wait_in(buf, slot):
         pltpu.make_async_copy(buf, buf, sem_r.at[slot]).wait()
 
-    def swap(src, dst, to, slot):
+    def swap(src, dst, y, slot):
         return pltpu.make_async_remote_copy(
             src, dst, sem_xs.at[slot], sem_xr.at[slot],
-            device_id=(me, to), device_id_type=MESH,
+            device_id=(y * size + place, ch), device_id_type=MESH,
         )
 
     for i in range(5):
@@ -144,11 +137,11 @@
     wabt[0:feat, :] = wa_f.T.astype(bf16)
     wabt[feat : 2 * feat, :] = wb_f.T.astype(bf16)
     ng[...] = jnp.broadcast_to(column(ngain[...]), (feat, cols))
-    place = lax.broadcasted_iota(jnp.int32, (rows, cols), 1)
+    lane = lax.broadcasted_iota(jnp.int32, (rows, cols), 1)
     step = lax.broadcasted_iota(jnp.int32, (rows, cols), 0)
     near = mask[pl.ds(me * rows // cols, 1), :].astype(f32)
     mask_rows = jnp.sum(
-        jnp.where(place == step + me * rows % cols, near, 0.0), axis=1, keepdims=True
+        jnp.where(lane == step + me * rows % cols, near, 0.0), axis=1, keepdims=True
     )
     pmask[...] = mask_rows * mask[pl.ds(ch, 1), :].astype(f32)
 
@@ -179,7 +172,7 @@
     lax.fori_loop(0, rows, forward, 0)
     s1b[...] = st_b[...].reshape(groups, rows, cols).astype(bf16)
     s1a[...] = st_a[...].reshape(groups, rows, cols).astype(bf16)
-    pl.semaphore_wait(barrier, groups + 2 - at_home.astype(jnp.int32))
+    pl.semaphore_wait(barrier, groups - 1 + 3)
     send_out(s1b, r1b, 0)
     send_out(s1a, r1a, 1)
 
@@ -204,54 +197,35 @@
     def unpack(buf):
         return buf[...].astype(f32).reshape(planes, block, cols).astype(bf16)
 
-    halves = (pl.ds(0, 2), pl.ds(2, 2))
-
-    def beside(buf, slot):
-        return swap(buf.at[ch], buf.at[ch], sib, slot)
-
-    def onward(buf, k, slot):
-        return swap(buf.at[ch, halves[k]], buf.at[ch, halves[k]], nei, slot + 1 + k)
-
-    def relay(buf, k, slot):
-        return swap(buf.at[nei, halves[k]], buf.at[nei, halves[k]], sib, slot + 3 + k)
-
-    def spread(buf, slot):
-        onward(buf, 0, slot).start()
-        onward(buf, 1, slot).start()
-        beside(buf, slot).start()
-
-    def pass_on(buf, slot):
-        for k in (0, 1):
-            onward(buf, k, slot).wait_recv()
-            relay(buf, k, slot).start()
+    others = (ahead, behind, across)
+
+    def spread(buf, w, slot):
+        return swap(buf.at[my_y], buf.at[my_y], (behind, ahead, across)[w], slot + w)
 
     wait_in(r1b, 0)
-    rf[ch] = unpack(r1b)
-    spread(rf, 0)
+    rf[my_y] = unpack(r1b)
+    for w in range(3):
+        spread(rf, w, 0).start()
 
     wait_in(r1a, 1)
-    lf[ch] = unpack(r1a)
+    lf[my_y] = unpack(r1a)
 
     def triangle(c):
         total = 0.0
         for k in range(planes):
             total += lax.dot_general(
-                lf[ch, k], rf[c, k], (((1,), (1,)), ((), ())), preferred_element_type=f32
+                lf[my_y, k], rf[c, k], (((1,), (1,)), ((), ())), preferred_element_type=f32
             )
         s2[c] = total.reshape(size, rows, cols).astype(bf16)
         send_back(s2, r2, c, 2)
 
-    triangle(ch)
-    pass_on(rf, 0)
-    beside(rf, 0).wait_recv()
-    triangle(sib)
-    triangle(nei)
-    relay(rf, 0, 0).wait_recv()
-    relay(rf, 1, 0).wait_recv()
-    triangle(diag)
-
-    spread(lf, 5)
-    pass_on(lf, 5)
+    triangle(my_y)
+    for w in range(3):
+        spread(rf, w, 0).wait_recv()
+        triangle(others[w])
+
+    for w in range(3):
+        spread(lf, w, 3).start()
 
     wait_in(r2, 2)
     st_a[...] = r2[...].astype(f32).reshape(tokens, cols)
@@ -280,17 +254,13 @@
     lax.fori_loop(0, rows, outputs, 0)
     pltpu.make_async_copy(upd, upd_h, sem_o.at[0]).start()
 
-    beside(lf, 5).wait_recv()
-    relay(lf, 0, 5).wait_recv()
-    relay(lf, 1, 5).wait_recv()
-
     def trade(w):
-        t = (diag, nei, sib)[w]
-        return swap(g.at[t], gt.at[ch], t, 10 + w)
+        y = (across, behind, ahead)[w]
+        return swap(g.at[y], gt.at[my_y], y, 6 + w)
 
     wait_in(r3, 3)
     g[...] = unpack(r3)
-    for w in (0, 1, 2):
+    for w in range(3):
         trade(w).start()
     for c in range(planes):
         total = mm(g[0], rf[0, c])
@@ -299,11 +269,13 @@
         s4a[c] = total.reshape(size, rows, cols).astype(bf16)
         send_back(s4a, r4a, c, 4)
 
-    gtt[...] = g[ch].astype(f32).T.astype(bf16)
+    for w in range(3):
+        spread(lf, w, 3).wait_recv()
+    gtt[...] = g[my_y].astype(f32).T.astype(bf16)
     for c in range(planes):
-        gr[c] = mm(gtt[...], lf[ch, c])
-    for w in (2, 1, 0):
-        t = (diag, nei, sib)[w]
+        gr[c] = mm(gtt[...], lf[my_y, c])
+    for w in (1, 2, 0):
+        t = (across, ahead, behind)[w]
         trade(w).wait_recv()
         gtt[...] = gt[t].astype(f32).T.astype(bf16)
         for c in range(planes):
@@ -340,22 +312,11 @@
     lax.fori_loop(0, rows, backward, 0)
 
     for slot in range(6):
-
-        @pl.when(at_home)
-        def _():
-            some = s3.at[pl.ds(0, groups - 1)]
-            pltpu.make_async_copy(some, some, sem_s.at[slot]).wait()
-
-        @pl.when(ch != my_y)
-        def _():
-            pltpu.make_async_copy(s3, s3, sem_s.at[slot]).wait()
-
-    for buf, slot in ((rf, 0), (lf, 5)):
-        beside(buf, slot).wait_send()
-        for k in (0, 1):
-            onward(buf, k, slot).wait_send()
-            relay(buf, k, slot).wait_send()
-    for w in (0, 1, 2):
+        some = s3.at[pl.ds(0, groups - 1)]
+        pltpu.make_async_copy(some, some, sem_s.at[slot]).wait()
+    for w in range(3):
+        spread(rf, w, 0).wait_send()
+        spread(lf, w, 3).wait_send()
         trade(w).wait_send()
     pltpu.make_async_copy(upd, upd_h, sem_o.at[0]).wait()
     pltpu.make_async_copy(pgrad, pgrad_h, sem_o.at[1]).wait()
@@ -393,7 +354,7 @@
         V(4, cols, cols),
         V(4, groups // 4, rows, cols, dtype=bf16), V(4, groups // 4, rows, cols, dtype=bf16),
         V(groups, rows, cols, dtype=bf16), V(groups, rows, cols, dtype=bf16),
-        dma((9,)), dma((2,)), dma((6,)), dma((6,)), dma((13,)), dma((13,)),
+        dma((9,)), dma((2,)), dma((6,)), dma((6,)), dma((9,)), dma((9,)),
     ]
     out = jax.ShapeDtypeStruct(pair.shape, bf16)
     return pl.pallas_call(

time: 59.7 us -> 56.2 us (0.941)
  Pallas kernels: 56.5 us -> 53 us
    pallas_call x1, Pallas kernels: 56.5 us -> 53 us  [local(): pl.pallas_call(kernel, out_shape=(out, out), in_specs=[hbm] * 9, out_spec...]
where the time goes in v7:
time: 56.2 us; the launch traced here: 56.1 us
  Pallas kernels  53 us (94%)
  local copies, waits for them, and re-layouts  2.42 us (4%)
  between operations  0.65 us (1%)
    pallas_call x1, Pallas kernels, local(): pl.pallas_call(kernel, out_shape=(out, out), in_specs=[hbm] * 9, out_spec...  53 us
    unnamed x4, local copies, waits for them, and re-layouts  2.42 us

profile of v7, /device:TPU:1, one launch (start us, length us, event | category | flops | bytes accessed | tf_op | source)
XLA Modules:
  0.0 56.1 jit_solution(14169948405960482698)
XLA Ops:
  0.6 53.0 %shard_map.104 = (bf16[8,128,128]{2,1,0:T(8,128)(2,1)}, bf16[8,128,128]{2,1,0:T(8,128)(2,1)}) custom-call(bf16[8,128,128]{2,1,0:T(8,128)(2,1)} %pair_h.1, s32[4,128]{1,0:T(4,128)} %bitcast.3, f32[1,128]{1,0:T(1,128)} %bitcast.4, bf16[128,128]{1,0:T(8,128)(2,1)} %wa_h.1, bf16[128,128]{1,0:T(8,128)(2,1)} %wb_h.1, bf16[128,128]{1,0:T(8,128)(2,1)} %wg_h.1, ...), custom_call_target="tpu_custom_call" | custom-call | tf_op jit(solution)/shard_map/pallas_call | solution.py:360
  53.7 0.0 copy-start
  53.7 1.7 %copy.13 = bf16[8,128,128]{2,1,0:T(8,128)(2,1)} copy(bf16[8,128,128]{2,1,0:T(8,128)(2,1)} %get-tuple-element.4) | data formatting | bytes 524288
  55.4 0.0 copy-done
  55.4 0.7 %copy.14 = bf16[8,128,128]{2,1,0:T(8,128)(2,1)} copy(bf16[8,128,128]{2,1,0:T(8,128)(2,1)S(1)} %copy-done) | data formatting | bytes 524288
Async XLA Ops:
  53.7 1.7 %copy-start = (bf16[8,128,128]{2,1,0:T(8,128)(2,1)S(1)}, bf16[8,128,128]{2,1,0:T(8,128)(2,1)}, u32[]{:S(2)}) copy-start(bf16[8,128,128]{2,1,0:T(8,128)(2,1)} %get-tuple-element.5) | copy-start | bytes 786436

commit v8 on v7

--- a/solution.py
+++ b/solution.py
@@ -32,7 +32,7 @@
     wabt, wgt, wot, ng, hg,
     normed, pinv, zn, proj, gate, cgate, qs, mq, xn, gz,
     st_a, st_b,
-    s1a, s1b, r1a, r1b, lf, rf, s2, r2, s3, r3, g, gt, gtt, gr, s4a, s4b, r4a, r4b,
+    s1a, s1b, r1a, r1b, lf, rf, s2, r2, s3, r3, r3t, g, s4a, s4b, r4a, r4b,
     sem_i, sem_o, sem_s, sem_r, sem_xs, sem_xr,
 ):
     rows, cols, feat = pair.shape
@@ -121,6 +121,33 @@
         @pl.when(c != ch)
         def _():
             post(src.at[c, place], to, place, c, slot)
+
+    def send_across(src, dst, slot):
+        to = dst.at[me]
+
+        def go(w, c):
+            pltpu.make_async_remote_copy(
+                src.at[c * size + w], to, sem_s.at[slot], sem_r.at[slot],
+                device_id=(ch * size + w, c), device_id_type=MESH,
+            ).start()
+
+        def one(u, _):
+            w = within(u)
+            for c in chans:
+                go(w, c)
+            return 0
+
+        lax.fori_loop(0, size - 1, one, 0)
+        for c in chans[1:]:
+            go(place, c)
+
+        @pl.when(ch == my_y)
+        def _():
+            keep(src.at[mine], to, slot)
+
+        @pl.when(ch != my_y)
+        def _():
+            go(place, ch)
 
     def wait_in(buf, slot):
         pltpu.make_async_copy(buf, buf, sem_r.at[slot]).wait()
@@ -241,9 +268,10 @@
         st_b[pl.ds(r, hid, stride=rows), :] = grad
         return 0
 
-    lax.fori_loop(0, rows, middle, 0)
+    lax.fori_loop(0, rows, middle, 0, unroll=8)
     s3[...] = st_b[...].reshape(groups, rows, cols).astype(bf16)
     send_out(s3, r3, 3)
+    send_across(s3, r3t, 6)
 
     def outputs(r, _):
         y = mm(wot[...], xn[r])
@@ -254,14 +282,8 @@
     lax.fori_loop(0, rows, outputs, 0)
     pltpu.make_async_copy(upd, upd_h, sem_o.at[0]).start()
 
-    def trade(w):
-        y = (across, behind, ahead)[w]
-        return swap(g.at[y], gt.at[my_y], y, 6 + w)
-
     wait_in(r3, 3)
     g[...] = unpack(r3)
-    for w in range(3):
-        trade(w).start()
     for c in range(planes):
         total = mm(g[0], rf[0, c])
         for k in range(1, planes):
@@ -271,20 +293,16 @@
 
     for w in range(3):
         spread(lf, w, 3).wait_recv()
-    gtt[...] = g[my_y].astype(f32).T.astype(bf16)
+    wait_in(r3t, 6)
+    for q in range(planes):
+        grad = r3t[q * size : (q + 1) * size].astype(f32).reshape(block, cols)
+        g[q] = grad.T.astype(bf16)
     for c in range(planes):
-        gr[c] = mm(gtt[...], lf[my_y, c])
-    for w in (1, 2, 0):
-        t = (across, ahead, behind)[w]
-        trade(w).wait_recv()
-        gtt[...] = gt[t].astype(f32).T.astype(bf16)
-        for c in range(planes):
-            total = gr[c] + mm(gtt[...], lf[t, c])
-            if w:
-                gr[c] = total
-            else:
-                s4b[c] = total.reshape(size, rows, cols).astype(bf16)
-                send_back(s4b, r4b, c, 5)
+        total = mm(g[0], lf[0, c])
+        for q in range(1, planes):
+            total += mm(g[q], lf[q, c])
+        s4b[c] = total.reshape(size, rows, cols).astype(bf16)
+        send_back(s4b, r4b, c, 5)
 
     wait_in(r4a, 4)
     st_a[...] = r4a[...].astype(f32).reshape(tokens, cols)
@@ -295,7 +313,7 @@
         gz[r] += mm(wa[...], d)
         return 0
 
-    lax.fori_loop(0, rows, left_back, 0)
+    lax.fori_loop(0, rows, left_back, 0, unroll=8)
     wait_in(r4b, 5)
     st_b[...] = r4b[...].astype(f32).reshape(tokens, cols)
 
@@ -309,17 +327,45 @@
         pltpu.make_async_copy(pgrad.at[r], pgrad_h.at[r], sem_o.at[1]).start()
         return 0
 
-    lax.fori_loop(0, rows, backward, 0)
+    lax.fori_loop(0, rows, backward, 0, unroll=8)
 
     for slot in range(6):
         some = s3.at[pl.ds(0, groups - 1)]
         pltpu.make_async_copy(some, some, sem_s.at[slot]).wait()
+
+    @pl.when(ch == my_y)
+    def _():
+        some = s3.at[pl.ds(0, groups - 1)]
+        pltpu.make_async_copy(some, some, sem_s.at[6]).wait()
+
+    @pl.when(ch != my_y)
+    def _():
+        pltpu.make_async_copy(s3, s3, sem_s.at[6]).wait()
+
     for w in range(3):
         spread(rf, w, 0).wait_send()
         spread(lf, w, 3).wait_send()
-        trade(w).wait_send()
     pltpu.make_async_copy(upd, upd_h, sem_o.at[0]).wait()
     pltpu.make_async_copy(pgrad, pgrad_h, sem_o.at[1]).wait()
+
+
+def hand_out(a, b, a_out, b_out, a_held, b_held, sem_in, sem_out):
+    half = a.shape[0] // 2
+
+    def pieces(sources, targets, sem):
+        for n in range(4):
+            at = pl.ds(n // 2 * half, half)
+            yield pltpu.make_async_copy(sources[n % 2].at[at], targets[n % 2].at[at], sem.at[n])
+
+    inward = list(pieces((a, b), (a_held, b_held), sem_in))
+    outward = list(pieces((a_held, b_held), (a_out, b_out), sem_out))
+    for copy in inward:
+        copy.start()
+    for arriving, leaving in zip(inward, outward):
+        arriving.wait()
+        leaving.start()
+    for copy in outward:
+        copy.wait()
 
 
 def local(pair, token_mask, norm_gain, w_a, w_b, w_gate, hid_gain, w_out, cotangent):
@@ -350,14 +396,13 @@
         V(4, 4, cols, cols, dtype=bf16), V(4, 4, cols, cols, dtype=bf16),
         V(4, groups // 4, rows, cols, dtype=bf16), V(groups, rows, cols, dtype=bf16),
         V(groups, rows, cols, dtype=bf16), V(4, groups // 4, rows, cols, dtype=bf16),
-        V(4, cols, cols, dtype=bf16), V(4, cols, cols, dtype=bf16), V(cols, cols, dtype=bf16),
-        V(4, cols, cols),
+        V(groups, rows, cols, dtype=bf16), V(4, cols, cols, dtype=bf16),
         V(4, groups // 4, rows, cols, dtype=bf16), V(4, groups // 4, rows, cols, dtype=bf16),
         V(groups, rows, cols, dtype=bf16), V(groups, rows, cols, dtype=bf16),
-        dma((9,)), dma((2,)), dma((6,)), dma((6,)), dma((9,)), dma((9,)),
+        dma((9,)), dma((2,)), dma((7,)), dma((7,)), dma((6,)), dma((6,)),
     ]
     out = jax.ShapeDtypeStruct(pair.shape, bf16)
-    return pl.pallas_call(
+    results = pl.pallas_call(
         kernel,
         out_shape=(out, out),
         in_specs=[hbm] * 9,
@@ -370,6 +415,16 @@
         pair, token_mask.reshape(tokens // cols, cols), norm_gain.reshape(1, feat),
         w_a, w_b, w_gate, hid_gain.reshape(1, hid), w_out, cotangent,
     )
+    return pl.pallas_call(
+        hand_out,
+        out_shape=(out, out),
+        in_specs=[hbm, hbm],
+        out_specs=(hbm, hbm),
+        scratch_shapes=[
+            V(rows, cols, feat, dtype=bf16), V(rows, cols, feat, dtype=bf16), dma((4,)), dma((4,)),
+        ],
+        compiler_params=pltpu.CompilerParams(vmem_limit_bytes=56 << 20),
+    )(*results)
 
 
 def solution(mesh):

time: 56.2 us -> 53.2 us (0.947)
  local copies, waits for them, and re-layouts: 2.42 us -> 0 us
  Pallas kernels: 53 us -> 52.4 us
    pallas_call x1, Pallas kernels: 53 us -> 50.6 us  [local(): pl.pallas_call(kernel, out_shape=(out, out), in_specs=[hbm] * 9, out_spec...]
    unnamed x4 -> x0, local copies, waits for them, and re-layouts: 2.42 us -> none
    pallas_call x0 -> x1, Pallas kernels: none -> 1.82 us  [local(): pl.pallas_call(hand_out, out_shape=(out, out), in_specs=[hbm, hbm], out_s...]
where the time goes in v8:
time: 53.2 us; the launch traced here: 53 us
  Pallas kernels  52.4 us (98%)
  between operations  0.64 us (1%)
    pallas_call x1, Pallas kernels, local(): pl.pallas_call(kernel, out_shape=(out, out), in_specs=[hbm] * 9, out_spec...  50.6 us
    pallas_call x1, Pallas kernels, local(): pl.pallas_call(hand_out, out_shape=(out, out), in_specs=[hbm, hbm], out_s...  1.82 us

profile of v8, /device:TPU:1, one launch (start us, length us, event | category | flops | bytes accessed | tf_op | source)
XLA Modules:
  0.0 53.0 jit_solution(4761121079381996394)
XLA Ops:
  0.6 50.6 %shard_map.104 = (bf16[8,128,128]{2,1,0:T(8,128)(2,1)}, bf16[8,128,128]{2,1,0:T(8,128)(2,1)}) custom-call(bf16[8,128,128]{2,1,0:T(8,128)(2,1)} %pair_h.1, s32[4,128]{1,0:T(4,128)} %bitcast.3, f32[1,128]{1,0:T(1,128)} %bitcast.4, bf16[128,128]{1,0:T(8,128)(2,1)} %wa_h.1, bf16[128,128]{1,0:T(8,128)(2,1)} %wb_h.1, bf16[128,128]{1,0:T(8,128)(2,1)} %wg_h.1, ...), custom_call_target="tpu_custom_call" | custom-call | tf_op jit(solution)/shard_map/pallas_call | solution.py:405
  51.2 1.8 %shard_map.105 = (bf16[8,128,128]{2,1,0:T(8,128)(2,1)}, bf16[8,128,128]{2,1,0:T(8,128)(2,1)}) custom-call(bf16[8,128,128]{2,1,0:T(8,128)(2,1)} %get-tuple-element.4.a, bf16[8,128,128]{2,1,0:T(8,128)(2,1)} %get-tuple-element.5.b), custom_call_target="tpu_custom_call" | custom-call | tf_op jit(solution)/shard_map/pallas_call | solution.py:418

commit v9 on v8

--- a/solution.py
+++ b/solution.py
@@ -32,8 +32,8 @@
     wabt, wgt, wot, ng, hg,
     normed, pinv, zn, proj, gate, cgate, qs, mq, xn, gz,
     st_a, st_b,
-    s1a, s1b, r1a, r1b, lf, rf, s2, r2, s3, r3, r3t, g, s4a, s4b, r4a, r4b,
-    sem_i, sem_o, sem_s, sem_r, sem_xs, sem_xr,
+    s1a, s1b, r1a, r1b, r1x, lf, rf, s2, r2, s3, r3, r3t, g, gtt, s4a, s4b, r4a, r4b,
+    sem_i, sem_o, sem_s, sem_r, sem_xs, sem_xr, ready,
 ):
     rows, cols, feat = pair.shape
     hid = wo.shape[0]
@@ -122,32 +122,17 @@
         def _():
             post(src.at[c, place], to, place, c, slot)
 
-    def send_across(src, dst, slot):
-        to = dst.at[me]
-
-        def go(w, c):
-            pltpu.make_async_remote_copy(
-                src.at[c * size + w], to, sem_s.at[slot], sem_r.at[slot],
-                device_id=(ch * size + w, c), device_id_type=MESH,
-            ).start()
-
+    def send_over(src, to, y, slot):
         def one(u, _):
             w = within(u)
             for c in chans:
-                go(w, c)
+                pltpu.make_async_remote_copy(
+                    src.at[c * size + w], to, sem_s.at[slot], sem_r.at[slot],
+                    device_id=(y * size + w, c), device_id_type=MESH,
+                ).start()
             return 0
 
-        lax.fori_loop(0, size - 1, one, 0)
-        for c in chans[1:]:
-            go(place, c)
-
-        @pl.when(ch == my_y)
-        def _():
-            keep(src.at[mine], to, slot)
-
-        @pl.when(ch != my_y)
-        def _():
-            go(place, ch)
+        lax.fori_loop(0, size, one, 0)
 
     def wait_in(buf, slot):
         pltpu.make_async_copy(buf, buf, sem_r.at[slot]).wait()
@@ -200,7 +185,12 @@
     s1b[...] = st_b[...].reshape(groups, rows, cols).astype(bf16)
     s1a[...] = st_a[...].reshape(groups, rows, cols).astype(bf16)
     pl.semaphore_wait(barrier, groups - 1 + 3)
+    pl.semaphore_signal(
+        ready, inc=1, device_id=(across * size + place, ch), device_id_type=MESH
+    )
     send_out(s1b, r1b, 0)
+    pl.semaphore_wait(ready, 1)
+    send_over(s1b, r1x.at[ch, place], across, 7)
     send_out(s1a, r1a, 1)
 
     for i in range(5, 9):
@@ -231,7 +221,7 @@
 
     wait_in(r1b, 0)
     rf[my_y] = unpack(r1b)
-    for w in range(3):
+    for w in range(2):
         spread(rf, w, 0).start()
 
     wait_in(r1a, 1)
@@ -247,9 +237,12 @@
         send_back(s2, r2, c, 2)
 
     triangle(my_y)
-    for w in range(3):
+    for w in range(2):
         spread(rf, w, 0).wait_recv()
         triangle(others[w])
+    wait_in(r1x, 7)
+    rf[across] = unpack(r1x)
+    triangle(across)
 
     for w in range(3):
         spread(lf, w, 3).start()
@@ -271,7 +264,11 @@
     lax.fori_loop(0, rows, middle, 0, unroll=8)
     s3[...] = st_b[...].reshape(groups, rows, cols).astype(bf16)
     send_out(s3, r3, 3)
-    send_across(s3, r3t, 6)
+
+    @pl.when(ch != my_y)
+    def _():
+        send_over(s3, r3t.at[my_y, place], ch, 6)
+
 
     def outputs(r, _):
         y = mm(wot[...], xn[r])
@@ -293,14 +290,15 @@
 
     for w in range(3):
         spread(lf, w, 3).wait_recv()
-    wait_in(r3t, 6)
-    for q in range(planes):
-        grad = r3t[q * size : (q + 1) * size].astype(f32).reshape(block, cols)
-        g[q] = grad.T.astype(bf16)
+    gtt[0] = g[my_y].astype(f32).T.astype(bf16)
+    wait_in(r3t.at[pl.ds(0, planes - 1)], 6)
+    for n in range(3):
+        grad = r3t[others[n]].astype(f32).reshape(block, cols)
+        gtt[1 + n] = grad.T.astype(bf16)
     for c in range(planes):
-        total = mm(g[0], lf[0, c])
-        for q in range(1, planes):
-            total += mm(g[q], lf[q, c])
+        total = mm(gtt[0], lf[my_y, c])
+        for n in range(3):
+            total += mm(gtt[1 + n], lf[others[n], c])
         s4b[c] = total.reshape(size, rows, cols).astype(bf16)
         send_back(s4b, r4b, c, 5)
 
@@ -333,17 +331,15 @@
         some = s3.at[pl.ds(0, groups - 1)]
         pltpu.make_async_copy(some, some, sem_s.at[slot]).wait()
 
-    @pl.when(ch == my_y)
-    def _():
-        some = s3.at[pl.ds(0, groups - 1)]
-        pltpu.make_async_copy(some, some, sem_s.at[6]).wait()
+    pltpu.make_async_copy(s3, s3, sem_s.at[7]).wait()
 
     @pl.when(ch != my_y)
     def _():
         pltpu.make_async_copy(s3, s3, sem_s.at[6]).wait()
 
+    for w in range(2):
+        spread(rf, w, 0).wait_send()
     for w in range(3):
-        spread(rf, w, 0).wait_send()
         spread(lf, w, 3).wait_send()
     pltpu.make_async_copy(upd, upd_h, sem_o.at[0]).wait()
     pltpu.make_async_copy(pgrad, pgrad_h, sem_o.at[1]).wait()
@@ -392,14 +388,16 @@
         V(rows, feat, cols),
         V(tokens, cols), V(tokens, cols),
         V(groups, rows, cols, dtype=bf16), V(groups, rows, cols, dtype=bf16),
-        V(4, groups // 4, rows, cols, dtype=bf16), V(4, groups // 4, rows, cols, dtype=bf16),
+        *[V(4, groups // 4, rows, cols, dtype=bf16) for _ in range(3)],
         V(4, 4, cols, cols, dtype=bf16), V(4, 4, cols, cols, dtype=bf16),
         V(4, groups // 4, rows, cols, dtype=bf16), V(groups, rows, cols, dtype=bf16),
         V(groups, rows, cols, dtype=bf16), V(4, groups // 4, rows, cols, dtype=bf16),
-        V(groups, rows, cols, dtype=bf16), V(4, cols, cols, dtype=bf16),
+        V(4, groups // 4, rows, cols, dtype=bf16), V(4, cols, cols, dtype=bf16),
+        V(4, cols, cols, dtype=bf16),
         V(4, groups // 4, rows, cols, dtype=bf16), V(4, groups // 4, rows, cols, dtype=bf16),
         V(groups, rows, cols, dtype=bf16), V(groups, rows, cols, dtype=bf16),
-        dma((9,)), dma((2,)), dma((7,)), dma((7,)), dma((6,)), dma((6,)),
+        dma((9,)), dma((2,)), dma((8,)), dma((8,)), dma((6,)), dma((6,)),
+        pltpu.SemaphoreType.REGULAR,
     ]
     out = jax.ShapeDtypeStruct(pair.shape, bf16)
     results = pl.pallas_call(

time: 53.2 us -> 52.5 us (0.987)
  Pallas kernels: 52.4 us -> 51.8 us
    pallas_call x1, Pallas kernels: 50.6 us -> 50 us  [local(): pl.pallas_call(kernel, out_shape=(out, out), in_specs=[hbm] * 9, out_spec...]
where the time goes in v9:
time: 52.5 us; the launch traced here: 52.4 us
  Pallas kernels  51.8 us (99%)
  between operations  0.64 us (1%)
    pallas_call x1, Pallas kernels, local(): pl.pallas_call(kernel, out_shape=(out, out), in_specs=[hbm] * 9, out_spec...  50 us
    pallas_call x1, Pallas kernels, local(): pl.pallas_call(hand_out, out_shape=(out, out), in_specs=[hbm, hbm], out_s...  1.82 us

profile of v9, /device:TPU:1, one launch (start us, length us, event | category | flops | bytes accessed | tf_op | source)
XLA Modules:
  0.0 52.4 jit_solution(2284449063098871834)
XLA Ops:
  0.6 50.0 %shard_map.104 = (bf16[8,128,128]{2,1,0:T(8,128)(2,1)}, bf16[8,128,128]{2,1,0:T(8,128)(2,1)}) custom-call(bf16[8,128,128]{2,1,0:T(8,128)(2,1)} %pair_h.1, s32[4,128]{1,0:T(4,128)} %bitcast.3, f32[1,128]{1,0:T(1,128)} %bitcast.4, bf16[128,128]{1,0:T(8,128)(2,1)} %wa_h.1, bf16[128,128]{1,0:T(8,128)(2,1)} %wb_h.1, bf16[128,128]{1,0:T(8,128)(2,1)} %wg_h.1, ...), custom_call_target="tpu_custom_call" | custom-call | tf_op jit(solution)/shard_map/pallas_call | solution.py:403
  50.6 1.8 %shard_map.105 = (bf16[8,128,128]{2,1,0:T(8,128)(2,1)}, bf16[8,128,128]{2,1,0:T(8,128)(2,1)}) custom-call(bf16[8,128,128]{2,1,0:T(8,128)(2,1)} %get-tuple-element.4.a, bf16[8,128,128]{2,1,0:T(8,128)(2,1)} %get-tuple-element.5.b), custom_call_target="tpu_custom_call" | custom-call | tf_op jit(solution)/shard_map/pallas_call | solution.py:416

commit v10 on v9

--- a/solution.py
+++ b/solution.py
@@ -75,7 +75,7 @@
             signal(my_y * size + within(u), c)
         return 0
 
-    lax.fori_loop(0, size - 1, greet, 0)
+    lax.fori_loop(0, size - 1, greet, 0, unroll=True)
     for c in chans[1:]:
         signal(me, c)
     for y in (across, ahead, behind):
@@ -99,7 +99,7 @@
                 post(src.at[c * size + w], to, w, c, slot)
             return 0
 
-        lax.fori_loop(0, size - 1, one, 0)
+        lax.fori_loop(0, size - 1, one, 0, unroll=True)
         for c in chans[1:]:
             post(src.at[c * size + place], to, place, c, slot)
         keep(src.at[mine], to, slot)
@@ -112,7 +112,7 @@
             post(src.at[c, w], to, w, c, slot)
             return 0
 
-        lax.fori_loop(0, size - 1, one, 0)
+        lax.fori_loop(0, size - 1, one, 0, unroll=True)
 
         @pl.when(c == ch)
         def _():
@@ -133,6 +133,22 @@
             return 0
 
         lax.fori_loop(0, size, one, 0)
+
+    def send_early(src, dst, slot):
+        to = dst.at[mine]
+
+        def one(u, _):
+            w = u % 2 * 8 + u // 2
+            for c in range(planes):
+
+                @pl.when((w != place) | (ch != c))
+                def _():
+                    post(src.at[c, w], to, w, c, slot)
+
+            return 0
+
+        lax.fori_loop(0, size, one, 0)
+        keep(src.at[ch, place], to, slot)
 
     def wait_in(buf, slot):
         pltpu.make_async_copy(buf, buf, sem_r.at[slot]).wait()
@@ -300,7 +316,7 @@
         for n in range(3):
             total += mm(gtt[1 + n], lf[others[n], c])
         s4b[c] = total.reshape(size, rows, cols).astype(bf16)
-        send_back(s4b, r4b, c, 5)
+    send_early(s4b, r4b, 5)
 
     wait_in(r4a, 4)
     st_a[...] = r4a[...].astype(f32).reshape(tokens, cols)

time: 52.5 us -> 52.2 us (level)
  no operation moved by 1% of the time
where the time goes in v10:
time: 52.2 us; the launch traced here: 52.1 us
  Pallas kernels  51.4 us (98%)
  between operations  0.64 us (1%)
    pallas_call x1, Pallas kernels, local(): pl.pallas_call(kernel, out_shape=(out, out), in_specs=[hbm] * 9, out_spec...  49.6 us
    pallas_call x1, Pallas kernels, local(): pl.pallas_call(hand_out, out_shape=(out, out), in_specs=[hbm, hbm], out_s...  1.82 us

profile of v10, /device:TPU:1, one launch (start us, length us, event | category | flops | bytes accessed | tf_op | source)
XLA Modules:
  0.0 52.1 jit_solution(15279815696041813217)
XLA Ops:
  0.6 49.6 %shard_map.104 = (bf16[8,128,128]{2,1,0:T(8,128)(2,1)}, bf16[8,128,128]{2,1,0:T(8,128)(2,1)}) custom-call(bf16[8,128,128]{2,1,0:T(8,128)(2,1)} %pair_h.1, s32[4,128]{1,0:T(4,128)} %bitcast.3, f32[1,128]{1,0:T(1,128)} %bitcast.4, bf16[128,128]{1,0:T(8,128)(2,1)} %wa_h.1, bf16[128,128]{1,0:T(8,128)(2,1)} %wb_h.1, bf16[128,128]{1,0:T(8,128)(2,1)} %wg_h.1, ...), custom_call_target="tpu_custom_call" | custom-call | tf_op jit(solution)/shard_map/pallas_call | solution.py:419
  50.3 1.8 %shard_map.105 = (bf16[8,128,128]{2,1,0:T(8,128)(2,1)}, bf16[8,128,128]{2,1,0:T(8,128)(2,1)}) custom-call(bf16[8,128,128]{2,1,0:T(8,128)(2,1)} %get-tuple-element.4.a, bf16[8,128,128]{2,1,0:T(8,128)(2,1)} %get-tuple-element.5.b), custom_call_target="tpu_custom_call" | custom-call | tf_op jit(solution)/shard_map/pallas_call | solution.py:432

commit v11 on v10

--- a/solution.py
+++ b/solution.py
@@ -312,9 +312,10 @@
         grad = r3t[others[n]].astype(f32).reshape(block, cols)
         gtt[1 + n] = grad.T.astype(bf16)
     for c in range(planes):
-        total = mm(gtt[0], lf[my_y, c])
-        for n in range(3):
-            total += mm(gtt[1 + n], lf[others[n], c])
+        total = mm(
+            jnp.concatenate([gtt[n] for n in range(planes)], axis=1),
+            jnp.concatenate([lf[my_y, c]] + [lf[others[n], c] for n in range(3)], axis=0),
+        )
         s4b[c] = total.reshape(size, rows, cols).astype(bf16)
     send_early(s4b, r4b, 5)
 

time: 52.2 us -> 52.2 us (level)
  no operation moved by 1% of the time
where the time goes in v11:
time: 52.2 us; the launch traced here: 52.1 us
  Pallas kernels  51.4 us (98%)
  between operations  0.64 us (1%)
    pallas_call x1, Pallas kernels, local(): pl.pallas_call(kernel, out_shape=(out, out), in_specs=[hbm] * 9, out_spec...  49.6 us
    pallas_call x1, Pallas kernels, local(): pl.pallas_call(hand_out, out_shape=(out, out), in_specs=[hbm, hbm], out_s...  1.82 us

profile of v11, /device:TPU:1, one launch (start us, length us, event | category | flops | bytes accessed | tf_op | source)
XLA Modules:
  0.0 52.1 jit_solution(5549279131682998654)
XLA Ops:
  0.6 49.6 %shard_map.104 = (bf16[8,128,128]{2,1,0:T(8,128)(2,1)}, bf16[8,128,128]{2,1,0:T(8,128)(2,1)}) custom-call(bf16[8,128,128]{2,1,0:T(8,128)(2,1)} %pair_h.1, s32[4,128]{1,0:T(4,128)} %bitcast.3, f32[1,128]{1,0:T(1,128)} %bitcast.4, bf16[128,128]{1,0:T(8,128)(2,1)} %wa_h.1, bf16[128,128]{1,0:T(8,128)(2,1)} %wb_h.1, bf16[128,128]{1,0:T(8,128)(2,1)} %wg_h.1, ...), custom_call_target="tpu_custom_call" | custom-call | tf_op jit(solution)/shard_map/pallas_call | solution.py:420
  50.3 1.8 %shard_map.105 = (bf16[8,128,128]{2,1,0:T(8,128)(2,1)}, bf16[8,128,128]{2,1,0:T(8,128)(2,1)}) custom-call(bf16[8,128,128]{2,1,0:T(8,128)(2,1)} %get-tuple-element.4.a, bf16[8,128,128]{2,1,0:T(8,128)(2,1)} %get-tuple-element.5.b), custom_call_target="tpu_custom_call" | custom-call | tf_op jit(solution)/shard_map/pallas_call | solution.py:433
